TPU v7x, 128 devices: a whole 4x4x4 slice. The times are simulated.
128 devices in a mesh: section: 2 (over y_lo), dp: 32 (over x, z, core), fsdp: 2 (over y_hi).
Axes of the slice: x: 4, y: 4 (y_hi: 2, y_lo: 2; y = y_hi * 2 + y_lo), z: 4, core: 2. Of those that a mesh axis runs over, the one named last changes fastest.
Arguments:
- inputs: bfloat16 [8192, 1024], P(('dp', 'fsdp')), may hold values from -6 to 6
- out_grad: bfloat16 [8192, 1024], P(('dp', 'fsdp')), may hold values from -6 to 6
- doc_lengths: int32 [128], replicated, may hold values from 1 to 128, as said below
- doc_owner: int32 [128], replicated, may hold values from 0 to 63, as said below
- loss_mask: int32 [8192], P(('dp', 'fsdp')), may hold values 0 or 1
- gain_in: bfloat16 [2, 1024], P('section', 'fsdp'), may hold values from 0.099609375 to 1.8984375
- w_in: bfloat16 [2, 1024, 3072], P('section', 'fsdp'), may hold values from -0.1875 to 0.1875
- taps: bfloat16 [2, 2048, 4], P('section', 'fsdp'), may hold values from -3 to 3
- w_decay: bfloat16 [2, 1024, 8], P('section', 'fsdp'), may hold values from -0.1875 to 0.1875
- a_log: bfloat16 [2, 4], P('section', 'fsdp'), may hold values from -4 to 0.5
- dt_bias: bfloat16 [2, 4], P('section', 'fsdp'), may hold values from -5 to -1
- gain_out: bfloat16 [2, 256], P('section', 'fsdp'), may hold values from 0.099609375 to 1.8984375
- w_out: bfloat16 [2, 1024, 1024], P('section', 'fsdp'), may hold values from -0.1875 to 0.1875
- gain_ff: bfloat16 [2, 1024], P('section', 'fsdp'), may hold values from 0.099609375 to 1.8984375
- w_ff_in: bfloat16 [2, 1024, 2816], P('section', 'fsdp'), may hold values from -0.1875 to 0.1875
- w_down: bfloat16 [2, 1408, 1024], P('section', 'fsdp'), may hold values from -0.15625 to 0.15625
Outputs:
- hidden_states: bfloat16 [2, 8192, 1024], P('section', ('dp', 'fsdp'))
- input_grads: bfloat16 [2, 8192, 1024], P('section', ('dp', 'fsdp'))
- grad_gain_in: float32 [2, 1024], P('section', 'fsdp')
- grad_w_in: float32 [2, 1024, 3072], P('section', 'fsdp')
- grad_taps: float32 [2, 2048, 4], P('section', 'fsdp')
- grad_w_decay: float32 [2, 1024, 8], P('section', 'fsdp')
- grad_a_log: float32 [2, 4], P('section', 'fsdp')
- grad_dt_bias: float32 [2, 4], P('section', 'fsdp')
- grad_gain_out: float32 [2, 256], P('section', 'fsdp')
- grad_w_out: float32 [2, 1024, 1024], P('section', 'fsdp')
- grad_gain_ff: float32 [2, 1024], P('section', 'fsdp')
- grad_w_ff_in: float32 [2, 1024, 2816], P('section', 'fsdp')
- grad_w_down: float32 [2, 1408, 1024], P('section', 'fsdp')
Inputs may be any that keep to these rules, and one draw needn't show every extreme that they name: `doc_lengths`: the documents of one replica have lengths that sum to between 64 and 128; some replica holds a single document of length exactly 128. A replica may hold no document. `doc_owner`: any number of documents may go to one replica.
All inputs are finite; a program needn't handle non-finite values. No bound on the sum of `loss_mask` on one device may be relied on, other than what follows from the above.
Results may differ from a plain program's by a relative error of at most 0.03.
Values may be sent and summed in bfloat16 or wider, within the bound.
A program may use at most 256 MiB of HBM per device.

v0:
```python
import math

import jax
import jax.numpy as jnp
from jax import lax
from jax.sharding import PartitionSpec as P

HEADS = 4
KEY_DIM = 128
VALUE_DIM = 256
HIDDEN_FF = 1408
TAPS = 4
GROUP = 64


EPSILON = 1e-06
FINEST_PRECISION = lax.Precision.HIGHEST


def sent_together(arrays, axis, dim, along):
    widths = [math.prod(a.shape[along:]) for a in arrays]
    both = jnp.concatenate(
        [a.reshape(*a.shape[:along], w) for a, w in zip(arrays, widths)], axis=along
    )
    whole = lax.all_gather(both, axis, axis=dim, tiled=True)
    blocks = jnp.split(whole, [sum(widths[:k]) for k in range(1, len(widths))], axis=along)
    return tuple(
        (b.reshape(*whole.shape[:along], *a.shape[along:]) for a, b in zip(arrays, blocks))
    )


def side_by_side(arrays, axis, dim, along):
    ends, at = ([], 0)
    for a in arrays[:-1]:
        at += a.shape[along]
        ends.append(at)
    both = jnp.concatenate(arrays, axis=along)
    return tuple(jnp.split(lax.all_gather(both, axis, axis=dim, tiled=True), ends, axis=along))


def shifted(block, axis, distance):
    devices = range(lax.axis_size(axis))
    route = [(i - distance, i) for i in devices if i - distance in devices]
    return lax.ppermute(block, axis, route)


def in_blocks(x, dim, peers):
    before, after = (x.shape[:dim], x.shape[dim + 1 :])
    return jnp.moveaxis(x.reshape(*before, peers, -1, *after), dim, 0)


def summed_on_arrival(x, axis, dim):
    peers = lax.axis_size(axis)
    blocks = lax.all_to_all(in_blocks(x, dim, peers), axis, 0, 0, tiled=True)
    return jnp.sum(blocks.astype(jnp.float32), axis=0)


def side_by_side_2(arrays, axis, dim, along):
    widths = [a.shape[along] for a in arrays]
    both = jnp.concatenate(arrays, axis=along)
    whole = summed_on_arrival(both, axis, dim)
    return tuple(jnp.split(whole, [sum(widths[:k]) for k in range(1, len(widths))], axis=along))


def over_pieces(x, axis):
    blocks = lax.all_gather(x, axis)
    return blocks.sum(axis=0)


def doc_layout(doc_lengths, doc_owner, replica, length_dev):
    owned = (doc_owner == replica).astype(jnp.int32)
    doc_ends = jnp.cumsum(doc_lengths * owned, dtype=jnp.int32)
    places = jnp.arange(length_dev, dtype=jnp.int32)
    finished = (doc_ends[None, :] <= places[:, None]).astype(jnp.int32) * owned[None, :]
    segment = jnp.sum(finished, axis=1, dtype=jnp.int32)
    usable = (places < doc_ends[-1]).astype(jnp.int32)
    return (segment, usable)


def rms_scale(values, gain):
    return values * lax.rsqrt(jnp.mean(values * values, axis=-1, keepdims=True) + EPSILON) * gain


def delay_rows(values, offset):
    filler = jnp.zeros((offset,) + values.shape[1:], values.dtype)
    return jnp.concatenate([filler, values[:-offset]], axis=0)


def short_conv(signal, kernel, segment):
    result = signal * kernel[:, TAPS - 1]
    for offset in range(1, TAPS):
        earlier = jnp.concatenate([jnp.full((offset,), -1, jnp.int32), segment[:-offset]])
        linked = (earlier == segment).astype(jnp.float32)
        result = (
            result + delay_rows(signal, offset) * linked[:, None] * kernel[:, TAPS - 1 - offset]
        )
    return result


def delta_rule(queries, keys, values, betas, logdecay, segment):
    tokens_here = queries.shape[0]
    blocks = tokens_here // GROUP

    def split(array):
        return array.reshape((blocks, GROUP) + array.shape[1:])

    strict_lower = jnp.tril(jnp.ones((GROUP, GROUP), jnp.float32), -1)
    causal = jnp.tril(jnp.ones((GROUP, GROUP), jnp.float32), 0)
    identity = jnp.eye(GROUP, dtype=jnp.float32)

    def advance(carry, block):
        running_state, last_segment = carry
        query_block, key_block, value_block, beta_block, decay_block, segment_block = block
        summed = jnp.transpose(jnp.cumsum(decay_block, axis=0))
        same_doc = (segment_block[:, None] == segment_block[None, :]).astype(jnp.float32)
        spread = summed[:, :, None] - summed[:, None, :]
        weights_pair = jnp.exp(jnp.minimum(spread, 0.0)) * same_doc[None]
        per_head_keys = jnp.transpose(key_block, (1, 0, 2))
        per_head_queries = jnp.transpose(query_block, (1, 0, 2))
        value_heads = jnp.transpose(value_block, (1, 0, 2))
        beta_heads = jnp.transpose(beta_block)
        key_gram = jnp.einsum(
            "hik,hjk->hij", per_head_keys, per_head_keys, precision=FINEST_PRECISION
        )
        system = (
            identity[None] + beta_heads[:, :, None] * key_gram * weights_pair * strict_lower[None]
        )
        carried = (segment_block == last_segment).astype(jnp.float32)
        incoming_state = jnp.exp(summed) * carried[None, :]
        resolved_values = lax.linalg.triangular_solve(
            system,
            beta_heads[:, :, None] * value_heads,
            left_side=True,
            lower=True,
            unit_diagonal=True,
        )
        resolved_keys = lax.linalg.triangular_solve(
            system,
            (beta_heads * incoming_state)[:, :, None] * per_head_keys,
            left_side=True,
            lower=True,
            unit_diagonal=True,
        )
        state_updates = resolved_values - jnp.einsum(
            "rej,rjd->red", resolved_keys, running_state, precision=FINEST_PRECISION
        )
        scores = (
            jnp.einsum("hik,hjk->hij", per_head_queries, per_head_keys, precision=FINEST_PRECISION)
            * weights_pair
            * causal[None]
        )
        output_rows = jnp.einsum("hij,hjv->hiv", scores, state_updates, precision=FINEST_PRECISION)
        output_rows = output_rows + incoming_state[:, :, None] * jnp.einsum(
            "wru,wuq->wrq", per_head_queries, running_state, precision=FINEST_PRECISION
        )
        trailing_weight = (
            jnp.exp(jnp.minimum(summed[:, -1:] - summed, 0.0))
            * (segment_block == segment_block[-1]).astype(jnp.float32)[None, :]
        )
        updated_state = (carried[-1] * jnp.exp(summed[:, -1]))[:, None, None] * running_state
        updated_state = updated_state + jnp.einsum(
            "btu,btp->bup",
            trailing_weight[:, :, None] * per_head_keys,
            state_updates,
            precision=FINEST_PRECISION,
        )
        return ((updated_state, segment_block[-1]), jnp.transpose(output_rows, (1, 0, 2)))

    start = (jnp.zeros((HEADS, KEY_DIM, VALUE_DIM), jnp.float32), jnp.int32(-1))
    _, pieces = lax.scan(
        advance,
        start,
        (split(queries), split(keys), split(values), split(betas), split(logdecay), split(segment)),
    )
    return pieces.reshape(tokens_here, HEADS, VALUE_DIM)


def mixer_core(projected, decay_in, kernel, a_log, dt_bias, gain_out, segment):
    tokens_here = projected.shape[0]
    conv_width = 2 * HEADS * KEY_DIM + HEADS * VALUE_DIM
    convolved = jax.nn.silu(short_conv(projected[:, :conv_width], kernel, segment))
    queries = convolved[:, : HEADS * KEY_DIM].reshape(tokens_here, HEADS, KEY_DIM)
    keys = convolved[:, HEADS * KEY_DIM : 2 * HEADS * KEY_DIM].reshape(tokens_here, HEADS, KEY_DIM)
    values = convolved[:, 2 * HEADS * KEY_DIM :].reshape(tokens_here, HEADS, VALUE_DIM)
    queries = (
        queries
        * lax.rsqrt(jnp.sum(queries * queries, axis=-1, keepdims=True) + EPSILON)
        * KEY_DIM ** (-0.5)
    )
    keys = keys * lax.rsqrt(jnp.sum(keys * keys, axis=-1, keepdims=True) + EPSILON)
    betas = jax.nn.sigmoid(decay_in[:, HEADS:])
    logdecay = -jnp.exp(a_log) * jax.nn.softplus(decay_in[:, :HEADS] + dt_bias)
    delta = delta_rule(queries, keys, values, betas, logdecay, segment)
    normed = rms_scale(delta, gain_out)
    gate_part = jax.nn.silu(projected[:, conv_width:]).reshape(tokens_here, HEADS, VALUE_DIM)
    return (normed * gate_part).reshape(tokens_here, HEADS * VALUE_DIM)


def layer_forward(inputs, params, segment):
    gain_in, w_in, kernel, w_decay, a_log, dt_bias, gain_out, w_out, gain_ff, w_ff_in, w_down = (
        params
    )
    inputs_float = inputs.astype(jnp.float32)
    normed = rms_scale(inputs_float, gain_in.astype(jnp.float32)).astype(jnp.bfloat16)
    projected = jnp.dot(normed, w_in, preferred_element_type=jnp.float32)
    decay_in = jnp.dot(normed, w_decay, preferred_element_type=jnp.float32)
    mixed = mixer_core(
        projected,
        decay_in,
        kernel.astype(jnp.float32),
        a_log.astype(jnp.float32),
        dt_bias.astype(jnp.float32),
        gain_out.astype(jnp.float32),
        segment,
    ).astype(jnp.bfloat16)
    middle = inputs_float + jnp.dot(mixed, w_out, preferred_element_type=jnp.float32)
    normed_ff = rms_scale(middle, gain_ff.astype(jnp.float32)).astype(jnp.bfloat16)
    gate_up = jnp.dot(normed_ff, w_ff_in, preferred_element_type=jnp.float32)
    hidden = (jax.nn.silu(gate_up[:, :HIDDEN_FF]) * gate_up[:, HIDDEN_FF:]).astype(jnp.bfloat16)
    return (middle + jnp.dot(hidden, w_down, preferred_element_type=jnp.float32)).astype(
        jnp.bfloat16
    )


def layer_backward(inputs, params, segment, cotangent):
    gain_in, w_in, kernel, w_decay, a_log, dt_bias, gain_out, w_out, gain_ff, w_ff_in, w_down = (
        params
    )
    inputs_float = inputs.astype(jnp.float32)
    gain_in_f = gain_in.astype(jnp.float32)
    gain_ff_f = gain_ff.astype(jnp.float32)
    normed = rms_scale(inputs_float, gain_in_f).astype(jnp.bfloat16)
    projected = jnp.dot(normed, w_in, preferred_element_type=jnp.float32)
    decay_in = jnp.dot(normed, w_decay, preferred_element_type=jnp.float32)

    def mixer_piece(proj_arg, decay_arg, kernel_arg, alog_arg, bias_arg, gain_arg):
        return mixer_core(proj_arg, decay_arg, kernel_arg, alog_arg, bias_arg, gain_arg, segment)

    mixed_float, mixer_pull = jax.vjp(
        mixer_piece,
        projected,
        decay_in,
        kernel.astype(jnp.float32),
        a_log.astype(jnp.float32),
        dt_bias.astype(jnp.float32),
        gain_out.astype(jnp.float32),
    )
    mixed = mixed_float.astype(jnp.bfloat16)
    middle = inputs_float + jnp.dot(mixed, w_out, preferred_element_type=jnp.float32)
    normed_ff_float, norm_ff_pull = jax.vjp(rms_scale, middle, gain_ff_f)
    normed_ff = normed_ff_float.astype(jnp.bfloat16)
    gate_up = jnp.dot(normed_ff, w_ff_in, preferred_element_type=jnp.float32)
    gate_part = gate_up[:, :HIDDEN_FF]
    up_part = gate_up[:, HIDDEN_FF:]
    sigmoid_gate = jax.nn.sigmoid(gate_part)
    hidden = (gate_part * sigmoid_gate * up_part).astype(jnp.bfloat16)
    cot_rounded = cotangent.astype(jnp.bfloat16)
    grad_down = jnp.dot(hidden.T, cot_rounded, preferred_element_type=jnp.float32)
    d_hidden = jnp.dot(cot_rounded, w_down.T, preferred_element_type=jnp.float32)
    d_gate = d_hidden * up_part * sigmoid_gate * (1.0 + gate_part * (1.0 - sigmoid_gate))
    d_up = d_hidden * gate_part * sigmoid_gate
    d_gate_up = jnp.concatenate([d_gate, d_up], axis=1).astype(jnp.bfloat16)
    grad_ff_in = jnp.dot(normed_ff.T, d_gate_up, preferred_element_type=jnp.float32)
    d_normed_ff = jnp.dot(d_gate_up, w_ff_in.T, preferred_element_type=jnp.float32)
    d_middle_part, grad_gain_ff = norm_ff_pull(d_normed_ff)
    d_middle = cotangent + d_middle_part
    middle_rounded = d_middle.astype(jnp.bfloat16)
    grad_out = jnp.dot(mixed.T, middle_rounded, preferred_element_type=jnp.float32)
    d_mixed = jnp.dot(middle_rounded, w_out.T, preferred_element_type=jnp.float32)
    d_projected, d_decay_in, grad_kernel, grad_alog, grad_bias, grad_gain_out = mixer_pull(d_mixed)
    proj_rounded = d_projected.astype(jnp.bfloat16)
    decay_rounded = d_decay_in.astype(jnp.bfloat16)
    grad_in = jnp.dot(normed.T, proj_rounded, preferred_element_type=jnp.float32)
    grad_decay = jnp.dot(normed.T, decay_rounded, preferred_element_type=jnp.float32)
    d_normed = jnp.dot(proj_rounded, w_in.T, preferred_element_type=jnp.float32) + jnp.dot(
        decay_rounded, w_decay.T, preferred_element_type=jnp.float32
    )
    _, norm_in_pull = jax.vjp(rms_scale, inputs_float, gain_in_f)
    d_input_part, grad_gain_in = norm_in_pull(d_normed)
    d_inputs = d_middle + d_input_part
    grads = (
        grad_gain_in,
        grad_in,
        grad_kernel,
        grad_decay,
        grad_alog,
        grad_bias,
        grad_gain_out,
        grad_out,
        grad_gain_ff,
        grad_ff_in,
        grad_down,
    )
    return (d_inputs, grads)


def on_device(
    inputs,
    out_grad,
    doc_lengths,
    doc_owner,
    loss_mask,
    gain_in,
    w_in,
    taps,
    w_decay,
    a_log,
    dt_bias,
    gain_out,
    w_out,
    gain_ff,
    w_ff_in,
    w_down,
):
    section_index = lax.axis_index("section")
    pair_index = lax.axis_index("fsdp")
    pair_count = lax.axis_size("fsdp")
    replica = lax.axis_index("dp") * pair_count + pair_index
    segment, usable = doc_layout(doc_lengths, doc_owner, replica, inputs.shape[0])
    gathered = (
        *sent_together((gain_in, w_in), "fsdp", 1, 2),
        lax.all_gather(taps, "fsdp", axis=1, tiled=True),
        lax.all_gather(w_decay, "fsdp", axis=1, tiled=True),
        *side_by_side((a_log, dt_bias), "fsdp", 1, 0),
        lax.all_gather(gain_out, "fsdp", axis=1, tiled=True),
        *sent_together((w_out, gain_ff, w_ff_in), "fsdp", 1, 2),
        lax.all_gather(w_down, "fsdp", axis=1, tiled=True),
    )
    params = tuple((piece[0] for piece in gathered))
    zero_rows = jnp.zeros_like(inputs)
    first_out = lax.cond(
        section_index == 0, lambda: layer_forward(inputs, params, segment), lambda: zero_rows
    )
    received = shifted(first_out, "section", 1)
    section_out = lax.cond(
        section_index == 1, lambda: layer_forward(received, params, segment), lambda: first_out
    )
    zero_grads = tuple((jnp.zeros(param.shape, jnp.float32) for param in params))

    def backward_on(section_input, cotangent):
        d_inputs, grads = layer_backward(section_input, params, segment, cotangent)
        return (d_inputs.astype(jnp.bfloat16), grads)

    last_cot = out_grad.astype(jnp.float32) * (loss_mask * usable).astype(jnp.float32)[:, None]
    last_d, last_grads = lax.cond(
        section_index == 1, lambda: backward_on(received, last_cot), lambda: (zero_rows, zero_grads)
    )
    sent_back = shifted(last_d, "section", -1)
    section_d, grads = lax.cond(
        section_index == 0,
        lambda: backward_on(inputs, sent_back.astype(jnp.float32)),
        lambda: (last_d, last_grads),
    )
    matrices = (grads[1][None], grads[7][None], grads[9][None], grads[10][None])
    columns = (
        lax.psum_scatter(
            matrices[0].astype(jnp.bfloat16), "dp", scatter_dimension=2, tiled=True
        ).astype(jnp.float32),
        lax.psum_scatter(
            matrices[1].astype(jnp.bfloat16), "dp", scatter_dimension=2, tiled=True
        ).astype(jnp.float32),
        lax.psum_scatter(
            matrices[2].astype(jnp.bfloat16), "dp", scatter_dimension=2, tiled=True
        ).astype(jnp.float32),
        lax.psum_scatter(
            matrices[3].astype(jnp.bfloat16), "dp", scatter_dimension=2, tiled=True
        ).astype(jnp.float32),
    )
    shares = (
        *side_by_side_2(
            (
                columns[0].astype(jnp.bfloat16),
                columns[1].astype(jnp.bfloat16),
                columns[2].astype(jnp.bfloat16),
            ),
            "fsdp",
            1,
            2,
        ),
        summed_on_arrival(columns[3].astype(jnp.bfloat16), "fsdp", 1),
    )
    summed_mats = (
        lax.all_gather(shares[0].astype(jnp.bfloat16), "dp", axis=2, tiled=True).astype(
            jnp.float32
        ),
        lax.all_gather(shares[1].astype(jnp.bfloat16), "dp", axis=2, tiled=True).astype(
            jnp.float32
        ),
        lax.all_gather(shares[2].astype(jnp.bfloat16), "dp", axis=2, tiled=True).astype(
            jnp.float32
        ),
        lax.all_gather(shares[3].astype(jnp.bfloat16), "dp", axis=2, tiled=True).astype(
            jnp.float32
        ),
    )
    smalls = (
        over_pieces(grads[0], ("dp", "fsdp")),
        over_pieces(grads[2], ("dp", "fsdp")),
        over_pieces(grads[3], ("dp", "fsdp")),
        over_pieces(grads[4], ("dp", "fsdp")),
        over_pieces(grads[5], ("dp", "fsdp")),
        over_pieces(grads[6], ("dp", "fsdp")),
        over_pieces(grads[8], ("dp", "fsdp")),
    )

    def own_half(full):
        rows_here = full.shape[0] // pair_count
        return lax.dynamic_slice_in_dim(full, pair_index * rows_here, rows_here, 0)[None]

    return (
        section_out[None],
        section_d[None],
        own_half(smalls[0]),
        summed_mats[0],
        own_half(smalls[1]),
        own_half(smalls[2]),
        own_half(smalls[3]),
        own_half(smalls[4]),
        own_half(smalls[5]),
        summed_mats[1],
        own_half(smalls[6]),
        summed_mats[2],
        summed_mats[3],
    )


def solution(mesh):
    in_specs = (
        P(("dp", "fsdp"), None),
        P(("dp", "fsdp"), None),
        P(),
        P(),
        P(("dp", "fsdp")),
        P("section", "fsdp"),
        P("section", "fsdp", None),
        P("section", "fsdp", None),
        P("section", "fsdp", None),
        P("section", "fsdp"),
        P("section", "fsdp"),
        P("section", "fsdp"),
        P("section", "fsdp", None),
        P("section", "fsdp"),
        P("section", "fsdp", None),
        P("section", "fsdp", None),
    )
    out_specs = (
        P("section", ("dp", "fsdp"), None),
        P("section", ("dp", "fsdp"), None),
        P("section", "fsdp"),
        P("section", "fsdp", None),
        P("section", "fsdp", None),
        P("section", "fsdp", None),
        P("section", "fsdp"),
        P("section", "fsdp"),
        P("section", "fsdp"),
        P("section", "fsdp", None),
        P("section", "fsdp"),
        P("section", "fsdp", None),
        P("section", "fsdp", None),
    )
    return jax.shard_map(
        on_device, mesh=mesh, in_specs=in_specs, out_specs=out_specs, check_vma=False
    )
```

profile of v0, /device:TPU:8, one launch (start us, length us, event | category | flops | bytes accessed | tf_op | source)
XLA Modules:
  0.0 2149.1 jit_solution(9827493207549878849)
XLA Ops:
  8.1 5.1 pad_maximum_fusion.6
  15.0 7.0 concatenate.94
  23.9 5.7 all-gather.8
  29.8 6.0 all_gather.76
  35.8 6.1 all_gather.77
  41.9 5.7 all_gather.79
  48.8 53.7 %all-gather.20.cloned.1.call-done = bf16[1,1024,3073]{2,1,0:T(8,128)(2,1)} async-done(((bf16[1,512,3073]{2,1,0:T(8,128)(2,1)}), bf16[1,1024,3073]{2,1,0:T(8,128)(2,1)}) %all-gather.20.cloned.1.call-update) | async-done | bytes 6293520 | tf_op jit(solution)/shard_map/all_gather | solution.py:25
  103.6 8.7 slice_bitcast_fusion.6
  112.3 96.9 %all-gather.22.cloned.1.call-done = bf16[1,1024,3841]{2,1,0:T(8,128)(2,1)} async-done(((bf16[1,512,3841]{2,1,0:T(8,128)(2,1)}), bf16[1,1024,3841]{2,1,0:T(8,128)(2,1)}) %all-gather.22.cloned.1.call-update) | async-done | bytes 7866384 | tf_op jit(solution)/shard_map/all_gather | solution.py:25
  214.0 8.3 slice_bitcast_fusion.7
  222.3 34.1 %all-gather.24.cloned.1.call-done = bf16[1,1408,1024]{2,1,0:T(8,128)(2,1)} async-done(((bf16[1,704,1024]{2,1,0:T(8,128)(2,1)}), bf16[1,1408,1024]{2,1,0:T(8,128)(2,1)}) %all-gather.24.cloned.1.call-update) | async-done | bytes 2883600 | tf_op jit(solution)/shard_map/all_gather | solution.py:327
  261.8 108.4 %collective-permute-done = bf16[128,1024]{1,0:T(8,128)(2,1)S(1)} collective-permute-done((bf16[128,1024]{1,0:T(8,128)(2,1)}, bf16[128,1024]{1,0:T(8,128)(2,1)S(1)}, u32[]{:S(2)}, u32[]{:S(2)}) %collective-permute-start) | collective-permute-done | bytes 262176 | tf_op jit(solution)/shard_map/ppermute | solution.py:44
  370.9 315.4 %conditional.6 = (bf16[128,1024]{1,0:T(8,128)(2,1)}, f32[1024]{0:T(1024)}, bf16[1024,3072]{1,0:T(8,128)(2,1)}, f32[2048,4]{0,1:T(4,128)}, f32[1024,8]{0,1:T(8,12...) conditional(s32[]{:T(128)} %convert_element_type.420, ...), branch_computations={%region_22.25_spmd, %region_23.64_spmd} | conditional | flops 7678162944 | bytes 303733376 | solution.py:345
  372.2 3.8 fusion.269
  387.3 117.2 %while.244 = (s32[]{:T(128)}, f32[4,128,256]{2,1,0:T(8,128)S(1)}, s32[]{:T(128)}, f32[2,64,4,256]{3,1,2,0:T(8,128)}, f32[2,4,64,64]{3,2,1,0:T(8,128)}, /*index=5...) while((s32[]{:T(128)}, f32[4,128,256]{2,1,0:T(8,128)S(1)}, ...), condition=%wide.region_29.32_spmd.clone, body=%wide.region_27.31_spmd.clone.sunk | while | flops 479861632 | bytes 17990552 | solution.py:170
  395.9 19.7 custom-call.124
  454.4 19.7 custom-call.124
  508.8 3.8 fusion.266
  513.8 4.3 fusion.233
  533.6 119.6 %while.245 = (s32[]{:T(128)}, f32[4,128,256]{2,1,0:T(8,128)S(1)}, f32[2,64,4,128]{3,1,2,0:T(8,128)}, f32[2,64,4,128]{3,1,2,0:T(8,128)}, f32[2,64,4,256]{3,2,1,0:...) while((s32[]{:T(128)}, f32[4,128,256]{2,1,0:T(8,128)S(1)}, ...), condition=%wide.region_45.51_spmd.clone.clone, body=%wide.region_34.50_spmd.clone.clone.sunk | while | flops 984136256 | bytes 16748160 | solution.py:170
  538.9 19.7 custom-call.125
  598.5 19.7 custom-call.125
  674.2 4.5 fusion.247
  688.3 4.9 collective-permute-done.1
  693.2 7.6 conditional.7
  700.8 14.6 copy.1365
  715.4 10.9 copy.1362
  726.4 26.4 %copy.1410 = bf16[1,1024,2816]{1,0,2:T(2,128)(2,1)} copy(bf16[1,1024,2816]{2,1,0:T(8,128)(2,1)} %bitcast.1126) | data formatting | bytes 11534336
  752.8 9.2 copy.1661
  762.0 26.8 %copy.1408 = bf16[1,1024,3072]{1,0,2:T(2,128)(2,1)} copy(bf16[1,1024,3072]{2,1,0:T(8,128)(2,1)} %bitcast.1125) | data formatting | bytes 12582912
  788.9 9.8 copy.1660
  801.4 363.6 %all-reduce.60.cloned.1.call-done = (bf16[1,1024,1024]{1,0,2:T(2,128)(2,1)}, bf16[1,1408,1024]{1,0,2:T(2,128)(2,1)}) async-done(((bf16[1,1024,1024]{1,0,2:T(2,128)(2,1)}, bf16[1,1408,1024]{1,0,2:T(2,128)(2,1)}), (bf16[1,1024,1024]{1,0,2:T(2,128)(2,1)}, bf16[1,1408,1024]{1,0,2:T(2,128)(2,1)})) %all-reduce.60.cloned.1.call-update) | async-done | bytes 4980752
  1166.6 9.0 all_to_all.10
  1177.6 76.5 %reduce-scatter.9.cloned.1.call-done = bf16[88,1024]{1,0:T(8,128)(2,1)} async-done(((bf16[2816,1024]{1,0:T(8,128)(2,1)}), bf16[88,1024]{1,0:T(8,128)(2,1)}) %reduce-scatter.9.cloned.1.call-update) | async-done | bytes 180240
  1255.6 87.7 %reduce-scatter.7.cloned.1.call-done = bf16[96,1024]{1,0:T(8,128)(2,1)} async-done(((bf16[3072,1024]{1,0:T(8,128)(2,1)}), bf16[96,1024]{1,0:T(8,128)(2,1)}) %reduce-scatter.7.cloned.1.call-update) | async-done | bytes 196624
  1345.3 10.8 all_to_all.11
  1359.6 100.3 %conditional.5 = (bf16[1,128,1024]{2,1,0:T(8,128)(2,1)S(1)}) conditional(s32[]{:T(128)} %convert_element_type.420, bf16[128,1024]{1,0:T(8,128)(2,1)S(1)} %copy-done.81, (bf16[128,1024]{1,0:T(8,128)(2,1)S(1)}, bf16[1024]{0:T(1024)(128)(2,1)S(1)}, bf16[1024,3072]{1,0:T(8,128)(2,1)}, bf16[2048,4]{0,1:T(4,128)(2,1)S(1)}, s32[128]{0:T(128)S(1)}, ...), branch_computations={%region_12.15_spmd, %region_13.24_spmd} | conditional | flops 2671713280 | bytes 75941968 | solution.py:335
  1360.4 3.8 fusion.646
  1382.5 69.0 %while.243 = (s32[]{:T(128)}, f32[4,128,256]{2,1,0:T(8,128)S(1)}, s32[]{:T(128)}, f32[2,64,4,256]{3,1,2,0:T(8,128)}, s32[2,64]{1,0:T(2,128)}, /*index=5*/f32[2,6...) while((s32[]{:T(128)}, f32[4,128,256]{2,1,0:T(8,128)S(1)}, ...), condition=%wide.region_19.21_spmd.clone, body=%wide.region_17.20_spmd.clone.sunk | while | flops 479426176 | bytes 6822308 | solution.py:170
  1386.6 19.7 custom-call.126
  1421.1 19.7 custom-call.126
  1455.5 3.8 fusion.640
  1461.7 163.0 %all-reduce.56 = (f32[256]{0:T(256)S(1)}, f32[256]{0:T(256)S(1)}) all-reduce(f32[256]{0:T(256)S(1)} %dynamic-update-slice, f32[256]{0:T(256)S(1)} %dynamic-update-slice.1), channel_id=5, replica_groups=mesh['section'=2,'dp'=32,'fsdp'=2] {'dp','fsdp'}, use_global_device_ids=true, to_apply=%add.52 | all-reduce | flops 512 | bytes 4096
  1624.9 165.2 %all-gather.6 = f32[65536]{0:T(1024)S(1)} all-gather(f32[1024]{0:T(1024)} %get-tuple-element.3148), channel_id=8, replica_groups=mesh['section'=2,'dp'=32,'fsdp'=2] {'dp','fsdp'}, dimensions={0}, use_global_device_ids=true | all-gather | bytes 266240 | tf_op jit(solution)/shard_map/all_gather | solution.py:66
  1790.2 161.8 %all-gather = f32[65536]{0:T(1024)S(1)} all-gather(f32[1024]{0:T(1024)} %get-tuple-element.3139), channel_id=2, replica_groups=mesh['section'=2,'dp'=32,'fsdp'=2] {'dp','fsdp'}, dimensions={0}, use_global_device_ids=true | all-gather | bytes 266240 | tf_op jit(solution)/shard_map/all_gather | solution.py:66
  1953.5 164.2 %all-gather.9 = f32[64,1,256]{2,1,0:T(1,128)S(1)} all-gather(f32[1,1,256]{2,1,0:T(1,128)} %bitcast.72), channel_id=7, replica_groups=mesh['section'=2,'dp'=32,'fsdp'=2] {'dp','fsdp'}, dimensions={0}, use_global_device_ids=true | all-gather | bytes 66560 | tf_op jit(solution)/shard_map/all_gather | solution.py:66
  2131.2 5.2 copy.1369
  2136.3 5.4 copy.1367
  (782 shorter events, 314.7 us)
Async XLA Ops:
  7.2 95.3 %all-gather.20.cloned.1.call-start = ((), (), s32[]{:S(2)}) async-start(), calls=%async_computation.4 | async-start | bytes 9830400 | tf_op jit(solution)/shard_map/all_gather | solution.py:25
  13.2 196.1 %all-gather.22.cloned.1.call-start = ((), (), s32[]{:S(2)}) async-start(), calls=%async_computation.5 | async-start | bytes 12189696 | tf_op jit(solution)/shard_map/all_gather | solution.py:25
  22.0 13.8 copy-start.148
  22.0 19.9 copy-start.192
  22.1 234.3 %all-gather.24.cloned.1.call-start = ((), (), s32[]{:S(2)}) async-start(), calls=%async_computation.6 | async-start | bytes 4325376 | tf_op jit(solution)/shard_map/all_gather | solution.py:327
  22.8 1142.2 %all-reduce.60.cloned.1.call-start = ((), (), s32[]{:S(2)}) async-start(), calls=%async_computation.15 | async-start | bytes 19922944
  35.8 334.4 %copy-start.72 = (bf16[1,2048,4]{1,2,0:T(4,128)(2,1)}, bf16[1,2048,4]{1,2,0:T(4,128)(2,1)S(1)}, u32[]{:S(2)}) copy-start(bf16[1,2048,4]{1,2,0:T(4,128)(2,1)S(1)} %all_gather.76) | copy-start | bytes 49156
  48.3 208.1 %copy-start.88 = (s32[128]{0:T(128)}, s32[128]{0:T(128)S(1)}, u32[]{:S(2)}) copy-start(s32[128]{0:T(128)S(1)} %select_reduce_fusion) | copy-start | bytes 1540
  103.6 152.8 %copy-start.114 = (bf16[1024]{0:T(1024)(128)(2,1)}, bf16[1024]{0:T(1024)(128)(2,1)S(1)}, u32[]{:S(2)}) copy-start(bf16[1024]{0:T(1024)(128)(2,1)S(1)} %slice_reduce_fusion.3) | copy-start | bytes 6148
  214.0 42.4 %copy-start.6 = (bf16[128,1024]{1,0:T(8,128)(2,1)S(1)}, bf16[128,1024]{1,0:T(8,128)(2,1)}, u32[]{:S(2)}) copy-start(bf16[128,1024]{1,0:T(8,128)(2,1)} %param.47) | copy-start | bytes 786436
  257.4 112.8 %collective-permute-start = (bf16[128,1024]{1,0:T(8,128)(2,1)}, bf16[128,1024]{1,0:T(8,128)(2,1)S(1)}, u32[]{:S(2)}, u32[]{:S(2)}) collective-permute-start(bf16[128,1024]{1,0:T(8,128)(2,1)} %copy-done.80), channel_id=1, source_target_pairs={{0,64},{1,65},{2,66},{3,67},{4,68},{5,69},{6,70},{7,71},{8,72},{9,... | collective-permute-start | bytes 786440 | tf_op jit(solution)/shard_map/ppermute | solution.py:44
  371.3 12.6 copy-start.12
  371.5 12.4 copy-start.141
  372.2 11.7 copy-start.76
  429.6 14.7 copy-start.51
  432.0 12.4 copy-start.122
  488.1 14.7 copy-start.51
  490.4 12.4 copy-start.122
  533.6 122.9 %copy-start.77 = (f32[1024]{0:T(1024)S(1)}, f32[1024]{0:T(1024)}, u32[]{:S(2)}) copy-start(f32[1024]{0:T(1024)} %copy-done.76) | copy-start | bytes 12292 | tf_op jit(solution)/shard_map/cond
  558.6 10.6 copy-start.149
  558.6 11.8 copy-start.123
  558.6 11.8 copy-start.124
  618.2 10.6 copy-start.149
  618.2 11.8 copy-start.123
  618.2 11.8 copy-start.124
  653.3 11.0 copy-start.134
  653.3 12.0 copy-start.54
  653.3 14.7 copy-start.130
  686.3 6.9 collective-permute-start.1
  726.3 527.7 %reduce-scatter.9.cloned.1.call-start = ((), (), s32[]{:S(2)}) async-start(), calls=%async_computation.14 | async-start | bytes 5947392
  762.0 581.3 %reduce-scatter.7.cloned.1.call-start = ((), (), s32[]{:S(2)}) async-start(), calls=%async_computation.13 | async-start | bytes 6488064
  798.6 1320.3 %all-gather.34.cloned.1.call-start = ((), (), s32[]{:S(2)}) async-start(), calls=%async_computation.11 | async-start | bytes 2129920 | tf_op jit(solution)/shard_map/all_gather | solution.py:66
  799.4 1321.9 %all-gather.32.cloned.1.call-start = ((), (), s32[]{:S(2)}) async-start(), calls=%async_computation.10 | async-start | bytes 2129920 | tf_op jit(solution)/shard_map/all_gather | solution.py:66
  800.1 1324.5 %all-gather.36.cloned.1.call-start = ((), (), s32[]{:S(2)}) async-start(), calls=%async_computation.12 | async-start | bytes 1622016 | tf_op jit(solution)/shard_map/all_gather | solution.py:392
  1176.3 952.3 %all-gather.28.cloned.1.call-start = ((), (), s32[]{:S(2)}) async-start(), calls=%async_computation.8 | async-start | bytes 1081344 | tf_op jit(solution)/shard_map/all_gather | solution.py:386
  1255.6 102.8 %copy-start.193 = (u32[128]{0:T(128)S(1)}, u32[128]{0:T(128)}, u32[]{:S(2)}) copy-start(u32[128]{0:T(128)} %constant.755) | copy-start | bytes 1540
  1255.6 104.0 %copy-start.11 = (bf16[128,1024]{1,0:T(8,128)(2,1)S(1)}, bf16[128,1024]{1,0:T(8,128)(2,1)}, u32[]{:S(2)}) copy-start(bf16[128,1024]{1,0:T(8,128)(2,1)} %copy-done.10) | copy-start | bytes 786436
  1255.6 104.0 %copy-start.73 = (bf16[1,2048,4]{1,2,0:T(4,128)(2,1)S(1)}, bf16[1,2048,4]{1,2,0:T(4,128)(2,1)}, u32[]{:S(2)}) copy-start(bf16[1,2048,4]{1,2,0:T(4,128)(2,1)} %copy-done.72) | copy-start | bytes 49156
  1255.6 104.0 %copy-start.81 = (bf16[128,1024]{1,0:T(8,128)(2,1)S(1)}, bf16[128,1024]{1,0:T(8,128)(2,1)}, u32[]{:S(2)}) copy-start(bf16[128,1024]{1,0:T(8,128)(2,1)} %copy-done.80) | copy-start | bytes 786436
  1255.6 104.0 %copy-start.89 = (s32[128]{0:T(128)S(1)}, s32[128]{0:T(128)}, u32[]{:S(2)}) copy-start(s32[128]{0:T(128)} %copy-done.88) | copy-start | bytes 1540
  1255.6 104.0 %copy-start.115 = (bf16[1024]{0:T(1024)(128)(2,1)S(1)}, bf16[1024]{0:T(1024)(128)(2,1)}, u32[]{:S(2)}) copy-start(bf16[1024]{0:T(1024)(128)(2,1)} %copy-done.114) | copy-start | bytes 6148
  1356.9 774.3 %all-gather.30.cloned.1.call-start = ((), (), s32[]{:S(2)}) async-start(), calls=%async_computation.9 | async-start | bytes 2973696 | tf_op jit(solution)/shard_map/all_gather | solution.py:389
  1357.6 778.7 %all-gather.26.cloned.1.call-start = ((), (), s32[]{:S(2)}) async-start(), calls=%async_computation.7 | async-start | bytes 3244032 | tf_op jit(solution)/shard_map/all_gather | solution.py:383
  1383.8 25.4 %copy-start.50 = (f32[64,64]{1,0:T(8,128)}, f32[64,64]{1,0:T(8,128)S(1)}, u32[]{:S(2)}) copy-start(f32[64,64]{1,0:T(8,128)S(1)} %get-tuple-element.7705) | copy-start | bytes 49156 | tf_op jit(solution)/shard_map/cond/branch_1_fun/while
  1384.6 24.6 %copy-start.40 = (f32[64,4]{1,0:T(8,128)}, f32[64,4]{1,0:T(8,128)S(1)}, u32[]{:S(2)}) copy-start(f32[64,4]{1,0:T(8,128)S(1)} %reduce_window_sum.84) | copy-start | bytes 3076 | tf_op jit(solution)/shard_map/cond/branch_1_fun/while
  1418.3 25.4 %copy-start.50 = (f32[64,64]{1,0:T(8,128)}, f32[64,64]{1,0:T(8,128)S(1)}, u32[]{:S(2)}) copy-start(f32[64,64]{1,0:T(8,128)S(1)} %get-tuple-element.7705) | copy-start | bytes 49156 | tf_op jit(solution)/shard_map/cond/branch_1_fun/while
  1419.2 24.6 %copy-start.40 = (f32[64,4]{1,0:T(8,128)}, f32[64,4]{1,0:T(8,128)S(1)}, u32[]{:S(2)}) copy-start(f32[64,4]{1,0:T(8,128)S(1)} %reduce_window_sum.84) | copy-start | bytes 3076 | tf_op jit(solution)/shard_map/cond/branch_1_fun/while
  1460.0 664.7 %copy-start.82 = (bf16[1,128,1024]{2,1,0:T(8,128)(2,1)}, bf16[1,128,1024]{2,1,0:T(8,128)(2,1)S(1)}, u32[]{:S(2)}) copy-start(bf16[1,128,1024]{2,1,0:T(8,128)(2,1)S(1)} %get-tuple-element.8427) | copy-start | bytes 786436
  (89 other events, 253.4 us)
Sparse Core Ops, SparseCore 0:
  13.3 89.1 all-gather.19
  104.7 104.4 all-gather.21
  210.9 45.4 all-gather.23
  726.5 438.5 all-reduce.59
  1169.1 84.9 reduce-scatter.8
  1257.6 85.6 reduce-scatter.6
  1346.9 66.1 all-gather.33
  1416.7 65.1 all-gather.31
  1484.4 40.9 all-gather.35
  1527.8 42.0 all-gather.27
  1572.4 44.2 all-gather.29
  1619.1 44.4 all-gather.25
where the time goes:
time: 2160 us; the launch traced here: 2150 us
  waiting for transfers between devices  828 us (38%)
  blocking collectives  698 us (32%)
  local copies, waits for them, and re-layouts  263 us (12%)
  other arithmetic  204 us (9%)
  matrix products  121 us (6%)
    unnamed x15, waiting for transfers between devices  530 us
    all_gather x3, blocking collectives, over_pieces(): blocks = lax.all_gather(x, axis)  491 us
    unnamed x1, blocking collectives  163 us
    all_gather x2, waiting for transfers between devices, sent_together(): whole = lax.all_gather(both, axis, axis=dim, tiled=True)  151 us
    ppermute x2, waiting for transfers between devices, shifted(): return lax.ppermute(block, axis, route)  113 us
    unnamed x68, local copies, waits for them, and re-layouts  99.2 us
    another operation x16, other arithmetic, advance(): lax.linalg.triangular_solve(system, beta_heads[:, :, None] * value_heads,...  79.4 us
  transfers between devices with their start and end apart: 14, of which 8 were waited for; matrix products, arithmetic and copies ran while one was open for 11% of the time, Pallas kernels for 0%

commit v1 on v0

v1 whole, which is shorter than its diff:
```python
import functools
import math

import jax
import jax.numpy as jnp
from jax import lax
from jax.experimental import pallas as pl
from jax.experimental.pallas import tpu as pltpu
from jax.sharding import PartitionSpec as P

WIDTH = 1024
HEADS = 4
KEY_DIM = 128
VALUE_DIM = 256
HIDDEN_FF = 1408
TAPS = 4
TOK = 128
PROJ = 3072
CONV = 2048
EPS = 1e-06
PACK = 80
F32 = jnp.float32
BF16 = jnp.bfloat16
HI = lax.Precision.HIGHEST
M_INV, M_FWD, M_BWD = 3, 3, None
VMEM_LIMIT = 58 * 1024 * 1024

R_GIN, R_GFF, R_GOUT, R_TAPS, R_WD, R_ALOG, R_BIAS = 0, 4, 8, 9, 41, 73, 74


def dot(a, b, dims, mode):
    if mode != 3:
        if mode is None:
            a, b = a.astype(BF16), b.astype(BF16)
        return lax.dot_general(a, b, dims, precision=mode, preferred_element_type=F32)
    a1, b1 = a.astype(BF16), b.astype(BF16)
    a2, b2 = (a - a1.astype(F32)).astype(BF16), (b - b1.astype(F32)).astype(BF16)
    one = functools.partial(lax.dot_general, dimension_numbers=dims, preferred_element_type=F32)
    return one(a1, b1) + (one(a1, b2) + one(a2, b1))


def nn(a, b, mode=None):
    return dot(a, b, (((1,), (0,)), ((), ())), mode)


def nt(a, b, mode=None):
    return dot(a, b, (((1,), (1,)), ((), ())), mode)


def tn(a, b, mode=None):
    return dot(a, b, (((0,), (0,)), ((), ())), mode)


def iota(dim, shape=(TOK, TOK)):
    return lax.broadcasted_iota(jnp.int32, shape, dim)


def sigmoid(v):
    return 1.0 / (1.0 + jnp.exp(-v))


def softplus(v):
    e = jnp.exp(-jnp.abs(v))
    u = 1.0 + e
    tail = jnp.where(u == 1.0, e, jnp.log(u) * e / jnp.where(u == 1.0, 1.0, u - 1.0))
    return jnp.maximum(v, 0.0) + tail


def lanes(sm, first, count):
    return jnp.concatenate(
        [sm[half, r : r + 1, :] for half in range(2) for r in range(first, first + count)],
        axis=1,
    )


def decay_weights(sm):
    rows = [lanes(sm, R_WD + 4 * i, 4) for i in range(8)]
    rows.append(jnp.zeros((TOK - 8, WIDTH), F32))
    return jnp.concatenate(rows, axis=0).astype(BF16)


def layout(lens, owner, replica):
    i, j = iota(0), iota(1)
    owned = (owner == replica).astype(F32)
    held = lens.astype(F32) * owned
    ends = jnp.sum(jnp.where(j <= i, held, 0.0), axis=1, keepdims=True)
    owned_col = jnp.sum(jnp.where(j == i, owned, 0.0), axis=1, keepdims=True)
    done = jnp.where(ends <= j.astype(F32), owned_col, 0.0)
    seg_row = jnp.sum(done, axis=0, keepdims=True)
    seg_col = jnp.sum(jnp.where(j == i, seg_row, 0.0), axis=1, keepdims=True)
    total = jnp.sum(held, axis=1, keepdims=True)
    t = iota(0, (TOK, 1)).astype(F32)
    usable = (t < total).astype(F32)
    return seg_col, seg_row, usable


def links(seg_col):
    wide = jnp.broadcast_to(seg_col, (TOK, TOK))
    t = iota(0)
    return [
        ((pltpu.roll(wide, d, 0) == wide) & (t >= d)).astype(F32)[:, :1] for d in range(1, TAPS)
    ]


def conv_tile(sig, taps_rows, link):
    out = sig * taps_rows[TAPS - 1]
    for d in range(1, TAPS):
        out = out + pltpu.roll(sig, d, 0) * link[d - 1] * taps_rows[TAPS - 1 - d]
    return out


def norm_rows(v):
    return lax.rsqrt(jnp.mean(v * v, axis=-1, keepdims=True) + EPS)


def decays(dec, sm):
    alog = sm[0, R_ALOG : R_ALOG + 1, :] + sm[1, R_ALOG : R_ALOG + 1, :]
    bias = sm[0, R_BIAS : R_BIAS + 1, :] + sm[1, R_BIAS : R_BIAS + 1, :]
    z = dec + bias
    rate = -jnp.exp(alog)
    logdecay = rate * softplus(z)
    tri = (iota(1) <= iota(0)).astype(F32)
    summed = nn(tri, logdecay, HI)
    return z, rate, logdecay, summed, sigmoid(dec)


def inverse(systems):
    i, j = iota(0), iota(1)
    eye = (i == j).astype(F32)
    low = i > j
    found = [eye - jnp.where(low & ((i // 2) == (j // 2)), a, 0.0) for a in systems]
    size = 2
    while size < TOK:
        mask = low & ((i // (2 * size)) == (j // (2 * size))) & ((i // size) != (j // size))
        inner = [nn(jnp.where(mask, a, 0.0), m, M_INV) for a, m in zip(systems, found)]
        found = [m - nn(m, b, M_INV) for m, b in zip(found, inner)]
        size *= 2
    return found


def head_inputs(proj, taps, link, h):
    out = []
    for first, width in (
        (KEY_DIM * h, KEY_DIM),
        (HEADS * KEY_DIM + KEY_DIM * h, KEY_DIM),
        (2 * HEADS * KEY_DIM + VALUE_DIM * h, VALUE_DIM),
    ):
        rows = [t[:, first : first + width] for t in taps]
        out.append((first, width, rows, conv_tile(proj[:, first : first + width], rows, link)))
    return out


WEIGHT_SHAPES = ((WIDTH, PROJ), (WIDTH, WIDTH), (WIDTH, 2 * HIDDEN_FF), (HIDDEN_FF, WIDTH))


def forward_body(
    x_ref, sm_ref, rows_of, out_ref, proj_ref, dec_ref, inv_ref, mid_ref, gu_ref,
    w_in, w_out, w_ff, w_down, mixed_ref, hid_ref, hook,
):
    seg_col, seg_row, _ = rows_of
    link = links(seg_col)
    same = (seg_col == seg_row).astype(F32)
    xf = x_ref[...].astype(F32)
    normed = (xf * norm_rows(xf) * lanes(sm_ref, R_GIN, 4)).astype(BF16)
    dec = nt(normed, decay_weights(sm_ref))
    dec_ref[...] = dec
    hook("in")

    @pl.loop(0, PROJ // 512)
    def _(c):
        cols = pl.ds(pl.multiple_of(c * 512, 512), 512)
        proj_ref[:, cols] = nn(normed, w_in[:, cols])

    z, rate, logdecay, summed, beta = decays(dec, sm_ref)
    summed_t = summed.T
    taps = [lanes(sm_ref, R_TAPS + 8 * k, 8) for k in range(TAPS)]
    i, j = iota(0), iota(1)
    strict = i > j
    kept, systems = [], []
    for h in range(HEADS):
        (_, _, _, qc), (_, _, _, kc), (_, _, _, vc) = head_inputs(proj_ref, taps, link, h)
        q, k, v = (c * sigmoid(c) for c in (qc, kc, vc))
        q = q * lax.rsqrt(jnp.sum(q * q, axis=-1, keepdims=True) + EPS) * KEY_DIM ** (-0.5)
        k = k * lax.rsqrt(jnp.sum(k * k, axis=-1, keepdims=True) + EPS)
        w = jnp.exp(jnp.minimum(summed[:, h : h + 1] - summed_t[h : h + 1, :], 0.0)) * same
        b = beta[:, HEADS + h : HEADS + h + 1]
        gram = nt(k, k, M_FWD)
        systems.append(jnp.where(strict, b * gram * w, 0.0))
        scores = jnp.where(i >= j, nt(q, k, M_FWD) * w, 0.0)
        kept.append((scores, b * v))
        hook(h)
    inv = inverse(systems)
    hook("inverse")
    gain_out = lanes(sm_ref, R_GOUT, 1)
    for h in range(HEADS):
        inv_ref[h] = inv[h]
        scores, bv = kept[h]
        delta = nn(scores, nn(inv[h], bv, M_FWD), M_FWD)
        cols = slice(VALUE_DIM * h, VALUE_DIM * (h + 1))
        gate = proj_ref[:, CONV + VALUE_DIM * h : CONV + VALUE_DIM * (h + 1)]
        mixed_ref[:, cols] = (
            delta * norm_rows(delta) * gain_out * (gate * sigmoid(gate))
        ).astype(BF16)
    hook("out")
    mid = xf + nn(mixed_ref[...], w_out[...])
    mid_ref[...] = mid
    normed_ff = (mid * norm_rows(mid) * lanes(sm_ref, R_GFF, 4)).astype(BF16)
    hook("ff")

    @pl.loop(0, HIDDEN_FF // 128)
    def _(c):
        a = pl.ds(pl.multiple_of(c * 128, 128), 128)
        b = pl.ds(pl.multiple_of(HIDDEN_FF + c * 128, 128), 128)
        gate = nn(normed_ff, w_ff[:, a])
        up = nn(normed_ff, w_ff[:, b])
        gu_ref[:, a] = gate
        gu_ref[:, b] = up
        hid_ref[:, a] = (gate * sigmoid(gate) * up).astype(BF16)

    hook("down")
    out_ref[...] = (mid + nn(hid_ref[...], w_down[...])).astype(BF16)


def backward_body(
    x_ref, cot_ref, sm_ref, rows_of,
    proj_ref, dec_ref, inv_ref, mid_ref, gu_ref,
    dx_ref, small_ref, nrm_t, mix_t, nff_t, hid_t, dproj_ref, dmid_ref, dgu_ref, dout_ref,
    w_in, w_out, w_ff, w_down, dmix_ref,
):
    i, j = iota(0), iota(1)
    seg_col, seg_row, _ = rows_of
    link = links(seg_col)
    same = (seg_col == seg_row).astype(F32)
    dout = cot_ref[...].astype(F32)
    doutb = dout.astype(BF16)
    dout_ref[...] = doutb
    small_ref[...] = jnp.zeros_like(small_ref)

    for c in range(HIDDEN_FF // 128):
        a = slice(c * 128, c * 128 + 128)
        b = slice(HIDDEN_FF + c * 128, HIDDEN_FF + c * 128 + 128)
        gate, up = gu_ref[:, a], gu_ref[:, b]
        sg = sigmoid(gate)
        d_hidden = nt(doutb, w_down[a, :])
        dgu_ref[:, a] = (d_hidden * up * sg * (1.0 + gate * (1.0 - sg))).astype(BF16)
        dgu_ref[:, b] = (d_hidden * gate * sg).astype(BF16)
        hid_t[a, :] = (gate * sg * up).T.astype(BF16)
    mid = mid_ref[...]
    r = norm_rows(mid)
    n = mid * r
    gain_ff = lanes(sm_ref, R_GFF, 4)
    nff_t[...] = (n * gain_ff).T.astype(BF16)

    @pl.loop(0, WIDTH // 256)
    def _(c):
        rows = pl.ds(pl.multiple_of(c * 256, 256), 256)
        dmix_ref[:, rows] = nt(dgu_ref[...], w_ff[rows, :])

    d = dmix_ref[...]
    put(small_ref, R_GFF, 4, jnp.sum(d * n, axis=0, keepdims=True))
    d = d * gain_ff
    dmid = dout + r * (d - n * jnp.mean(d * n, axis=-1, keepdims=True))
    dmidb = dmid.astype(BF16)
    dmid_ref[...] = dmidb
    dmix_ref[...] = nt(dmidb, w_out[...])

    z, rate, logdecay, summed, beta = decays(dec_ref[...], sm_ref)
    summed_t = summed.T
    taps = [lanes(sm_ref, R_TAPS + 8 * k, 8) for k in range(TAPS)]
    gain_out = lanes(sm_ref, R_GOUT, 1)
    strict, causal = i > j, i >= j
    d_gain_out = jnp.zeros((1, VALUE_DIM), F32)
    d_col = jnp.zeros((TOK, TOK), F32)
    d_row = jnp.zeros((TOK, TOK), F32)
    for h in range(HEADS):
        parts = head_inputs(proj_ref, taps, link, h)
        sig = [sigmoid(p[3]) for p in parts]
        qa, ka, v = (p[3] * s for p, s in zip(parts, sig))
        rq = lax.rsqrt(jnp.sum(qa * qa, axis=-1, keepdims=True) + EPS)
        rk = lax.rsqrt(jnp.sum(ka * ka, axis=-1, keepdims=True) + EPS)
        q = qa * rq * KEY_DIM ** (-0.5)
        k = ka * rk
        w = jnp.exp(jnp.minimum(summed[:, h : h + 1] - summed_t[h : h + 1, :], 0.0)) * same
        b = beta[:, HEADS + h : HEADS + h + 1]
        gram = nt(k, k, M_FWD)
        qk = nt(q, k, M_FWD)
        ws = jnp.where(strict, w, 0.0)
        wc = jnp.where(causal, w, 0.0)
        scores = qk * wc
        inv = inv_ref[h]
        u = nn(inv, b * v, M_FWD)
        delta = nn(scores, u, M_FWD)
        gcols = slice(CONV + VALUE_DIM * h, CONV + VALUE_DIM * (h + 1))
        vcols = slice(VALUE_DIM * h, VALUE_DIM * (h + 1))
        gate = proj_ref[:, gcols]
        sg = sigmoid(gate)
        si = gate * sg
        rd = norm_rows(delta)
        nd = delta * rd
        dm = dmix_ref[:, vcols]
        mix_t[vcols, :] = (nd * gain_out * si).T.astype(BF16)
        dproj_ref[:, gcols] = (dm * nd * gain_out * sg * (1.0 + gate * (1.0 - sg))).astype(BF16)
        dn = dm * si
        d_gain_out = d_gain_out + jnp.sum(dn * nd, axis=0, keepdims=True)
        dn = dn * gain_out
        ddelta = rd * (dn - nd * jnp.mean(dn * nd, axis=-1, keepdims=True))
        dscores = nt(ddelta, u, M_BWD)
        du = tn(scores, ddelta, M_BWD)
        dr = tn(inv, du, M_BWD)
        da = -nt(dr, u, M_BWD)
        dqk = dscores * wc
        dgram = da * b * ws
        pair = dqk * qk + dgram * gram
        dq = nn(dqk, k, M_BWD)
        dk = tn(dqk, q, M_BWD) + nn(dgram + dgram.T, k, M_BWD)
        dv = b * dr
        dbeta = jnp.sum(da * gram * ws, axis=1, keepdims=True) + jnp.sum(
            dr * v, axis=1, keepdims=True
        )
        d_col = jnp.where(j == h, jnp.sum(pair, axis=1, keepdims=True), d_col)
        d_col = jnp.where(j == HEADS + h, dbeta, d_col)
        d_row = jnp.where(i == h, jnp.sum(pair, axis=0, keepdims=True), d_row)
        dq = KEY_DIM ** (-0.5) * dq
        dqa = rq * dq - qa * (rq * rq * rq) * jnp.sum(dq * qa, axis=-1, keepdims=True)
        dka = rk * dk - ka * (rk * rk * rk) * jnp.sum(dk * ka, axis=-1, keepdims=True)
        for (first, width, rows, c), s, dact in zip(parts, sig, (dqa, dka, dv)):
            dc = dact * s * (1.0 + c * (1.0 - s))
            raw = proj_ref[:, first : first + width]
            total = dc * rows[TAPS - 1]
            put_taps(small_ref, TAPS - 1, first, jnp.sum(dc * raw, axis=0, keepdims=True))
            for dist in range(1, TAPS):
                dcl = dc * link[dist - 1]
                put_taps(
                    small_ref, TAPS - 1 - dist, first,
                    jnp.sum(dcl * pltpu.roll(raw, dist, 0), axis=0, keepdims=True),
                )
                total = total + pltpu.roll(dcl, TOK - dist, 0) * rows[TAPS - 1 - dist]
            dproj_ref[:, first : first + width] = total.astype(BF16)
    put(small_ref, R_GOUT, 1, d_gain_out)
    d_summed = d_col - d_row.T
    later = (j >= i).astype(F32)
    dlog = nn(later, d_summed, HI)
    dz = dlog * rate * sigmoid(z)
    head_lane = j < HEADS
    d_alog = jnp.sum(jnp.where(head_lane, dlog * logdecay, 0.0), axis=0, keepdims=True)
    d_bias = jnp.sum(jnp.where(head_lane, dz, 0.0), axis=0, keepdims=True)
    for half in range(2):
        small_ref[half, R_ALOG : R_ALOG + 1, :] = d_alog
        small_ref[half, R_BIAS : R_BIAS + 1, :] = d_bias
    ddec = jnp.where(
        head_lane, dz, jnp.where(j < 2 * HEADS, d_col * beta * (1.0 - beta), 0.0)
    ).astype(BF16)

    xf = x_ref[...].astype(F32)
    r = norm_rows(xf)
    n = xf * r
    gain_in = lanes(sm_ref, R_GIN, 4)
    normed = (n * gain_in).astype(BF16)
    nrm_t[...] = (n * gain_in).T.astype(BF16)
    gwd = tn(ddec, normed)
    for row in range(2 * HEADS):
        put(small_ref, R_WD + 4 * row, 4, gwd[row : row + 1, :])

    @pl.loop(0, WIDTH // 256)
    def _(c):
        rows = pl.ds(pl.multiple_of(c * 256, 256), 256)
        dmix_ref[:, rows] = nt(dproj_ref[...], w_in[rows, :])

    d = dmix_ref[...] + nn(ddec, decay_weights(sm_ref))
    put(small_ref, R_GIN, 4, jnp.sum(d * n, axis=0, keepdims=True))
    d = d * gain_in
    dx_ref[...] = (dmid + r * (d - n * jnp.mean(d * n, axis=-1, keepdims=True))).astype(BF16)


def put(ref, first, count, row):
    for half in range(2):
        for c in range(count):
            at = (half * count + c) * 128
            ref[half, first + c : first + c + 1, :] = row[:, at : at + 128]


def put_taps(ref, tap, first, row):
    for c in range(row.shape[1] // 128):
        block = first // 128 + c
        at = R_TAPS + 8 * tap + block % 8
        ref[block // 8, at : at + 1, :] = row[:, c * 128 : c * 128 + 128]


ORDERS = ((0, 1, 2, 3), (1, 0, 3, 2), (2, 3, 0, 1), (3, 2, 1, 0))
FLAT = (
    (2, 0, 768, 0, True), (2, 768, 768, 1, True), (2, 1536, 768, 3, True), (2, 2304, 512, 2, True),
    (3, 0, 1024, 2, False), (0, 0, 1024, 0, False), (0, 1024, 1024, 1, False),
    (0, 2048, 1024, 3, False), (1, 0, 256, 0, False), (1, 256, 512, 1, False),
    (1, 768, 256, 3, False),
)
DOWN = 3


class Place:
    def __init__(self):
        self.section = lax.axis_index("section")
        dp = lax.axis_index("dp")
        self.half = lax.axis_index("fsdp")
        x, z, core = dp // 8, (dp // 2) % 4, dp % 2
        self.core = core

        def at(x, z, core, half):
            return (self.section, (x * 4 + z) * 2 + core, half)

        xa, za = x + 1 - 2 * (x % 2), z + 1 - 2 * (z % 2)
        self.links = (
            at(xa, z, core, self.half),
            at(3 - x, z, core, self.half),
            at(x, za, core, self.half),
            at(x, 3 - z, core, self.half),
        )
        self.sibling = at(x, z, 1 - core, self.half)
        self.pair = at(x, z, core, 1 - self.half)
        self.other = (1 - self.section, dp, self.half)
        self.bits = ((x % 2 + x // 2) % 2, x // 2, (z % 2 + z // 2) % 2, z // 2)

    def greet(self, *more):
        barrier = pltpu.get_barrier_semaphore()
        everyone = (*self.links, self.sibling, self.pair, *more)
        for device in everyone:
            pl.semaphore_signal(
                barrier, inc=1, device_id=device, device_id_type=pl.DeviceIdType.MESH
            )
        pl.semaphore_wait(barrier, len(everyone))


class Chunk:
    def __init__(self, place, weight, first, width, flavor, pair_first=False):
        self.pair_first = pair_first
        self.weight, self.first, self.width, self.order = weight, first, width, ORDERS[flavor]
        self.bits = [place.bits[d] for d in self.order]
        self.partners = [place.links[d] for d in self.order]
        self.rows = 352 if weight == DOWN else 256

    def size(self, steps):
        if self.weight == DOWN:
            return (self.rows >> min(steps, 1), self.width >> max(steps - 1, 0))
        return (self.rows >> steps, self.width)

    def start(self, steps, other=False):
        row = col = 0
        for k in range(1, steps + 1):
            bit = self.bits[k - 1]
            if other and k == steps:
                bit = 1 - bit
            if self.weight == DOWN and k > 1:
                col = col + bit * self.size(k)[1]
            else:
                row = row + bit * self.size(k)[0]
        return row, col

    def window(self, steps, other=False, row0=0, col0=0):
        (row, col), (rows, cols) = self.start(steps, other), self.size(steps)
        row, col = row + row0, col + col0
        if not isinstance(row, int):
            row = pl.multiple_of(row, 16)
        if not isinstance(col, int):
            col = pl.multiple_of(col, 128)
        return pl.ds(row, rows), pl.ds(col, cols)


def send(src, dst, sems, k, device):
    copy = pltpu.make_async_remote_copy(
        src_ref=src, dst_ref=dst, send_sem=sems[0].at[k], recv_sem=sems[1].at[k],
        device_id=device, device_id_type=pl.DeviceIdType.MESH,
    )
    copy.start()
    return copy


HALF_ROWS = (512, 512, 512, 704)
COLUMNS = (PROJ, WIDTH, 2 * HIDDEN_FF, WIDTH)


GATHER_FLAT = tuple(
    c[:4] for c in sorted(FLAT, key=lambda c: (0, 3, 1, 2)[c[0]])
)
PAIR_LAG = 1.0


def in_order(stages, lag):
    found = []
    for n, c in enumerate(FLAT):
        for stage in range(stages):
            late = lag if c[4] and stage else 0.0
            found.append((stage + late, n, stage))
    return [(n, stage) for _, n, stage in sorted(found)]


PACKED = 0
STAGES = 6


def layers_kernel(
    x_ref, cot_ref, mask_ref, lens_ref, own_ref,
    gin_ref, gff_ref, gout_ref, taps_ref, wdec_ref, alog_ref, bias_ref, wi, wo, wf, wd,
    out_ref, dx_ref, small_ref, nrm_t, mix_t, nff_t, hid_t, dproj_ref, dmid_ref, dgu_ref, dout_ref,
    w_in, w_out, w_ff, w_down, sm_ref, pk_wide, pk_ref, pk_far, proj_ref, dec_ref, inv_ref,
    mid_ref, gu_ref, mixed_ref, hid_ref, dmix_ref, xin_ref, next_ref, cin_ref, back_ref,
    send_sem, recv_sem, local_sem,
):
    place = Place()
    pk_wide[...] = jnp.zeros_like(pk_wide)
    for ref, first, per_row in (
        (gin_ref, R_GIN, 4), (gff_ref, R_GFF, 4), (gout_ref, R_GOUT, 1), (taps_ref, R_TAPS, 8),
        (wdec_ref, R_WD, 4),
    ):
        rows = ref[...].astype(F32)
        for r in range(rows.shape[0]):
            for c in range(per_row):
                at = first + r * per_row + c
                pk_wide[at : at + 1, :] = rows[r : r + 1, c * 128 : c * 128 + 128]
    for ref, at in ((alog_ref, R_ALOG), (bias_ref, R_BIAS)):
        two = ref[...].astype(F32)
        none = jnp.zeros((1, 2), F32)
        pk_wide[at : at + 1, 0:2] = jnp.where(place.half == 0, two, none)
        pk_wide[at : at + 1, 2:4] = jnp.where(place.half == 0, none, two)
    pk_ref[...] = pk_wide[...].astype(BF16)
    sems = (send_sem, recv_sem)
    shards, whole = (wi, wo, wf, wd), (w_in, w_out, w_ff, w_down)
    chunks = [Chunk(place, *c) for c in GATHER_FLAT]
    count = len(chunks)
    first = {w: [n for n, c in enumerate(chunks) if c.weight == w] for w in range(4)}

    def make(src, dst, k, device):
        return pltpu.make_async_remote_copy(
            src_ref=src, dst_ref=dst, send_sem=sems[0].at[k], recv_sem=sems[1].at[k],
            device_id=device, device_id_type=pl.DeviceIdType.MESH,
        )

    def local(w):
        rows = HALF_ROWS[w]
        at = pl.ds(pl.multiple_of(place.half * rows, 16), rows)
        return pltpu.make_async_copy(shards[w], whole[w].at[at, :], local_sem.at[w])

    def stage_copy(n, stage):
        c = chunks[n]
        w, rows = c.weight, HALF_ROWS[c.weight]
        k = 1 + stage * count + n
        if stage == 0:
            src = shards[w].at[c.window(4, row0=place.core * c.rows, col0=c.first)]
            to = c.window(4, row0=place.half * rows + place.core * c.rows, col0=c.first)
            return make(src, whole[w].at[to], k, place.pair)
        row0 = (1 - place.half) * rows + place.core * c.rows
        block = whole[w].at[c.window(5 - stage, row0=row0, col0=c.first)]
        device = c.partners[4 - stage] if stage < 5 else place.sibling
        return make(block, block, k, device)

    def passed_on(ns, stage):
        for n in ns:
            stage_copy(n, stage - 1).wait_recv()
            stage_copy(n, stage).start()

    rest = first[1] + first[2] + first[3]

    def complete(w):
        for n in first[w]:
            stage_copy(n, STAGES - 1).wait_recv()
        local(w).wait()

    def gather_hook(point):
        if point == "in":
            for stage in range(1, 4):
                passed_on(first[0], stage)
                if stage == 1:
                    passed_on(rest, 1)
            passed_on(first[0], 4)
            passed_on(rest, 2)
            passed_on(first[0], 5)
            complete(0)
        elif point == 0:
            passed_on(rest, 3)
        elif point == 2:
            passed_on(rest, 4)
        elif point == "inverse":
            passed_on(rest, 5)
        elif point in ("out", "ff", "down"):
            complete({"out": 1, "ff": 2, "down": 3}[point])

    place.greet(place.other)
    packed = make(pk_ref, pk_far, PACKED, place.pair)
    packed.start()
    for w in (0, 1, 2, 3):
        for n in first[w]:
            stage_copy(n, 0).start()
        local(w).start()
    rows_of = layout(lens_ref[...], own_ref[...], lax.axis_index("dp") * 2 + place.half)
    packed.wait()
    sm_ref[place.half] = pk_ref[...].astype(F32)
    sm_ref[1 - place.half] = pk_far[...].astype(F32)
    xin_ref[...] = x_ref[...]
    forth = make(out_ref, next_ref, 1 + STAGES * count, place.other)
    back = make(dx_ref, back_ref, 2 + STAGES * count, place.other)
    section = place.section

    @pl.loop(0, 2)
    def _(turn):
        def hook(point):
            @pl.when(turn == 0)
            def _():
                gather_hook(point)

        forward_body(
            xin_ref, sm_ref, rows_of, out_ref, proj_ref, dec_ref, inv_ref, mid_ref, gu_ref,
            w_in, w_out, w_ff, w_down, mixed_ref, hid_ref, hook,
        )

        @pl.when(turn == 0)
        def _():
            forth.start()
            forth.wait()
            xin_ref[...] = jnp.where(section == 0, x_ref[...], next_ref[...])

    mask = jnp.sum(
        jnp.where(iota(0) == iota(1), mask_ref[...].astype(F32), 0.0), axis=1, keepdims=True
    )
    cin_ref[...] = (cot_ref[...].astype(F32) * (mask * rows_of[2])).astype(BF16)

    @pl.loop(0, 2)
    def _(turn):
        backward_body(
            xin_ref, cin_ref, sm_ref, rows_of,
            proj_ref, dec_ref, inv_ref, mid_ref, gu_ref,
            dx_ref, small_ref, nrm_t, mix_t, nff_t, hid_t, dproj_ref, dmid_ref, dgu_ref, dout_ref,
            w_in, w_out, w_ff, w_down, dmix_ref,
        )

        @pl.when(turn == 0)
        def _():
            back.start()
            back.wait()
            cin_ref[...] = jnp.where(section == 0, back_ref[...], cin_ref[...])

    for n in range(count):
        for stage in range(STAGES):
            stage_copy(n, stage).wait_send()


def layers(x, cot, mask, lens, own, smalls, weights):
    vm = pl.BlockSpec(memory_space=pltpu.VMEM)
    hbm = pl.BlockSpec(memory_space=pl.ANY)
    tokens = (TOK, WIDTH)
    shapes = [
        (tokens, BF16), (tokens, BF16), ((2, PACK, 128), F32), ((WIDTH, TOK), BF16),
        ((WIDTH, TOK), BF16), ((WIDTH, TOK), BF16), ((HIDDEN_FF, TOK), BF16), ((TOK, PROJ), BF16),
        (tokens, BF16), ((TOK, 2 * HIDDEN_FF), BF16), (tokens, BF16),
    ]
    scratch = [(s, BF16) for s in WEIGHT_SHAPES] + [
        ((2, PACK, 128), F32), ((PACK, 128), F32), ((PACK, 128), BF16), ((PACK, 128), BF16),
        ((TOK, PROJ), F32), ((TOK, TOK), F32), ((HEADS, TOK, TOK), F32), (tokens, F32),
        ((TOK, 2 * HIDDEN_FF), F32), (tokens, BF16), ((TOK, HIDDEN_FF), BF16), (tokens, F32),
        (tokens, BF16), (tokens, BF16), (tokens, BF16), (tokens, BF16),
    ]
    count = 3 + STAGES * len(GATHER_FLAT)
    return pl.pallas_call(
        layers_kernel,
        name="gather_and_layers",
        out_shape=[jax.ShapeDtypeStruct(s, d) for s, d in shapes],
        in_specs=[vm] * 12 + [hbm] * 4,
        out_specs=[vm] * len(shapes),
        scratch_shapes=[pltpu.VMEM(s, d) for s, d in scratch]
        + [
            pltpu.SemaphoreType.DMA((count,)),
            pltpu.SemaphoreType.DMA((count,)),
            pltpu.SemaphoreType.DMA((4,)),
        ],
        compiler_params=pltpu.CompilerParams(
            collective_id=1, has_side_effects=True, vmem_limit_bytes=VMEM_LIMIT
        ),
    )(x, cot, mask, lens, own, *smalls, *weights)


def reduce_kernel(
    lag, stages, small_ref, l_in, l_out, l_ff, l_down, r_in, r_out, r_ff, r_down,
    tot_ref, g_in, g_out, g_ff, g_down, *scratch,
):
    place = Place()
    lhs, rhs = (l_in, l_out, l_ff, l_down), (r_in, r_out, r_ff, r_down)
    grads = (g_in, g_out, g_ff, g_down)
    peer_l, peer_r = scratch[0:4], scratch[4:8]
    count = len(FLAT)
    parts, fins = scratch[8 : 8 + count], scratch[8 + count : 8 + 2 * count]
    scratch = scratch[8 + 2 * count :]
    arrived = [scratch[5 * n : 5 * n + 5] for n in range(count)]
    sums, sums_in, sums_pair, send_sem, recv_sem, local_sem = scratch[5 * count :]
    sems = (send_sem, recv_sem)
    ids = iter(range(10 * count + 18))
    place.greet()
    sent = []

    crossing = {}
    for w in (2, 3, 0, 1):
        rows = peer_l[w].shape[1]
        found = []
        for h in range(2):
            at = pl.multiple_of(HALF_ROWS[w] * h + (1 - place.core) * rows, 16)
            found.append(
                send(lhs[w].at[pl.ds(at, rows), :], peer_l[w].at[h], sems, next(ids), place.sibling)
            )
        found.append(send(rhs[w], peer_r[w], sems, next(ids), place.sibling))
        sent += found
        crossing[w] = found

    sums[0] = small_ref[...]
    steps = (place.sibling, *place.links)
    small_ids = [next(ids) for _ in range(6)]
    small = send(sums.at[0], sums_in.at[0], sems, small_ids[0], steps[0])
    sent.append(small)

    chunks = [Chunk(place, *c) for c in FLAT]
    last, local = {}, {}

    def product(n, first):
        c = chunks[n]
        w = c.weight
        if c.pair_first:
            half = 1 - place.half if first else place.half
            blocks, rows = [(half, 0)], c.rows
        else:
            offset = pl.multiple_of(c.start(1, first)[0], 16)
            blocks, rows = [(0, offset), (1, offset)], c.size(1)[0]
        left = []
        for h, offset in blocks:
            at = pl.multiple_of(HALF_ROWS[w] * h + place.core * c.rows + offset, 16)
            left.append(
                jnp.concatenate(
                    [lhs[w][pl.ds(at, rows), :], peer_l[w][h, pl.ds(offset, rows), :]], axis=1
                )
            )
        both = left[0] if len(left) == 1 else jnp.concatenate(left, axis=0)
        for t in range(0, c.width, 256):
            cols = slice(c.first + t, c.first + t + 256)
            right = jnp.concatenate([rhs[w][:, cols], peer_r[w][:, cols]], axis=0)
            out = nn(both, right).astype(BF16)
            for k, (h, offset) in enumerate(blocks):
                parts[n][h, pl.ds(offset, rows), t : t + 256] = out[k * rows : (k + 1) * rows]

    def halves(n):
        return place.half if chunks[n].pair_first else slice(None)

    def give(n, step):
        c = chunks[n]
        at = c.window(step, other=True)
        last[n] = send(
            parts[n].at[halves(n), at[0], at[1]], arrived[n][step - 1], sems, next(ids),
            c.partners[step - 1],
        )
        sent.append(last[n])

    def add(n, step):
        c = chunks[n]
        (row, col), (rows, cols) = c.start(step), c.size(step)
        col = pl.ds(pl.multiple_of(col, 128), cols) if c.weight == DOWN else slice(None)
        lead = (slice(None),) if not c.pair_first else ()

        @pl.loop(0, rows // 16)
        def _(t):
            at = pl.ds(pl.multiple_of(row + t * 16, 16), 16)
            got = arrived[n][step - 1][(*lead, pl.ds(pl.multiple_of(t * 16, 16), 16), slice(None))]
            old = parts[n][halves(n), at, col]
            parts[n][halves(n), at, col] = (old.astype(F32) + got.astype(F32)).astype(BF16)

    def finish(n, block):
        c = chunks[n]
        fins[n][...] = block
        to = grads[c.weight].at[c.window(4, row0=place.core * c.rows, col0=c.first)]
        local[n] = pltpu.make_async_copy(fins[n], to, local_sem.at[n])
        local[n].start()
        last[n] = send(fins[n], to, sems, next(ids), c.partners[3])
        sent.append(last[n])

    def to_pair(n, src, dst):
        last[n] = send(src, dst, sems, next(ids), place.pair)
        sent.append(last[n])

    for n, stage in in_order(stages, lag):
        c = chunks[n]
        w = c.weight
        if stage == 0:
            for copy in crossing.pop(w, ()):
                copy.wait_recv()
            product(n, True)
            if c.pair_first:
                to_pair(n, parts[n].at[1 - place.half], arrived[n][4])
            else:
                give(n, 1)
            product(n, False)
        elif c.pair_first and stage == 1:
            last[n].wait_recv()

            @pl.loop(0, c.rows // 16)
            def _(t):
                at = pl.ds(pl.multiple_of(t * 16, 16), 16)
                old = parts[n][place.half, at, :].astype(F32)
                parts[n][place.half, at, :] = (old + arrived[n][4][at, :].astype(F32)).astype(BF16)

            give(n, 1)
        elif c.pair_first and stage <= 4:
            last[n].wait_recv()
            add(n, stage - 1)
            give(n, stage)
        elif c.pair_first and stage == 5:
            last[n].wait_recv()
            at = c.window(4)
            finish(
                n,
                (
                    parts[n][place.half, at[0], at[1]].astype(F32)
                    + arrived[n][3][...].astype(F32)
                ).astype(BF16),
            )
        elif stage <= 3:
            last[n].wait_recv()
            add(n, stage)
            give(n, stage + 1)
        elif stage == 4:
            last[n].wait_recv()
            add(n, 4)
            at = c.window(4)
            to_pair(n, parts[n].at[1 - place.half, at[0], at[1]], arrived[n][4])
        elif stage == 5:
            last[n].wait_recv()
            at = c.window(4)
            finish(
                n,
                (
                    parts[n][place.half, at[0], at[1]].astype(F32)
                    + arrived[n][4][...].astype(F32)
                ).astype(BF16),
            )
        elif stage <= 8:
            if stage == 6:
                local[n].wait()
            last[n].wait_recv()
            steps_left = 9 - stage
            block = grads[w].at[c.window(steps_left, row0=place.core * c.rows, col0=c.first)]
            last[n] = send(block, block, sems, next(ids), c.partners[steps_left - 1])
            sent.append(last[n])
        else:
            last[n].wait_recv()
            block = grads[w].at[c.window(0, row0=place.core * c.rows, col0=c.first)]
            last[n] = send(block, block, sems, next(ids), place.sibling)
            sent.append(last[n])
        if stage == 0 and 1 <= n <= 5:
            small.wait_recv()
            sums[n] = sums[n - 1] + sums_in[n - 1]
            if n < 5:
                small = send(sums.at[n], sums_in.at[n], sems, small_ids[n], steps[n])
            else:
                small = send(
                    sums.at[5, 1 - place.half], sums_pair, sems, small_ids[5], place.pair
                )
            sent.append(small)
    small.wait_recv()
    tot_ref[...] = sums[5, place.half] + sums_pair[...]
    for n in range(count):
        last[n].wait_recv()
    for copy in sent:
        copy.wait_send()


class Sizes:
    bits = (0, 0, 0, 0)
    links = (None,) * 4


def reduce(small, lhs, rhs, lag=None, stages=10, cid=2):
    vm = pl.BlockSpec(memory_space=pltpu.VMEM)
    hbm = pl.BlockSpec(memory_space=pl.ANY)
    chunks = [Chunk(Sizes, *c) for c in FLAT]
    count = len(FLAT)
    scratch = [pltpu.VMEM((2, r // 2, TOK), BF16) for r in HALF_ROWS]
    scratch += [pltpu.VMEM((TOK, c), BF16) for c in COLUMNS]
    scratch += [pltpu.VMEM((2, *c.size(0)), BF16) for c in chunks]
    scratch += [pltpu.VMEM(c.size(4), BF16) for c in chunks]
    for c in chunks:
        lead = () if c.pair_first else (2,)
        scratch += [pltpu.VMEM((*lead, *c.size(k)), BF16) for k in range(1, 5)]
        scratch.append(pltpu.VMEM(c.size(0 if c.pair_first else 4), BF16))
    total = 10 * count + 18
    scratch += [
        pltpu.VMEM((6, 2, PACK, 128), F32),
        pltpu.VMEM((5, 2, PACK, 128), F32),
        pltpu.VMEM((PACK, 128), F32),
        pltpu.SemaphoreType.DMA((total,)),
        pltpu.SemaphoreType.DMA((total,)),
        pltpu.SemaphoreType.DMA((count,)),
    ]
    return pl.pallas_call(
        functools.partial(reduce_kernel, PAIR_LAG if lag is None else lag, stages),
        name="reduce_gradients",
        out_shape=[jax.ShapeDtypeStruct((PACK, 128), F32)]
        + [jax.ShapeDtypeStruct((r, c), BF16) for r, c in zip(HALF_ROWS, COLUMNS)],
        in_specs=[vm] * 9,
        out_specs=[vm] + [hbm] * 4,
        scratch_shapes=scratch,
        compiler_params=pltpu.CompilerParams(
            collective_id=cid, has_side_effects=True, vmem_limit_bytes=VMEM_LIMIT
        ),
    )(small, *lhs, *rhs)


def finish_kernel(tot_ref, *refs):
    sources, (o_gin, o_taps, o_wd, o_alog, o_bias, o_gout, o_gff) = refs[:4], refs[4:11]
    targets, narrow, wide = refs[11:15], refs[15:19], refs[19:23]
    in_sem, out_sem = refs[23:]
    half = lax.axis_index("fsdp")
    blocks = []
    for w, rows in enumerate(HALF_ROWS):
        size = rows // 4
        blocks += [(w, slice(k * size, (k + 1) * size)) for k in range(4)]
    loads = [
        pltpu.make_async_copy(sources[w].at[at], narrow[w].at[at], in_sem.at[k])
        for k, (w, at) in enumerate(blocks)
    ]
    for copy in loads:
        copy.start()

    def row(first, count):
        return jnp.concatenate([tot_ref[first + k : first + k + 1, :] for k in range(count)], 1)

    o_gin[...] = row(R_GIN, 4)
    o_gff[...] = row(R_GFF, 4)
    o_gout[...] = row(R_GOUT, 1)
    for k in range(TAPS):
        o_taps[k : k + 1, :] = row(R_TAPS + 8 * k, 8)
    for k in range(2 * HEADS):
        o_wd[k : k + 1, :] = row(R_WD + 4 * k, 4)
    for ref, at in ((o_alog, R_ALOG), (o_bias, R_BIAS)):
        both = row(at, 1)
        ref[...] = jnp.where(half == 0, both[:, 0:2], both[:, 2:4])
    stores = []
    for k, (w, at) in enumerate(blocks):
        loads[k].wait()
        first, count = at.start, at.stop - at.start

        @pl.loop(0, count // 16)
        def _(t):
            here = pl.ds(pl.multiple_of(first + t * 16, 16), 16)
            wide[w][here, :] = narrow[w][here, :].astype(F32)

        copy = pltpu.make_async_copy(wide[w].at[at], targets[w].at[at], out_sem.at[k])
        copy.start()
        stores.append(copy)
    for copy in stores:
        copy.wait()


def finished(total, grads):
    vm = pl.BlockSpec(memory_space=pltpu.VMEM)
    hbm = pl.BlockSpec(memory_space=pl.ANY)
    small = [(1, 512), (TAPS, 1024), (2 * HEADS, 512), (1, 2), (1, 2), (1, 128), (1, 512)]
    shapes = list(zip(HALF_ROWS, COLUMNS))
    return pl.pallas_call(
        finish_kernel,
        name="widen_gradients",
        out_shape=[jax.ShapeDtypeStruct(s, F32) for s in small + shapes],
        in_specs=[vm] + [hbm] * 4,
        out_specs=[vm] * 7 + [hbm] * 4,
        scratch_shapes=[pltpu.VMEM(s, BF16) for s in shapes]
        + [pltpu.VMEM(s, F32) for s in shapes]
        + [pltpu.SemaphoreType.DMA((16,)), pltpu.SemaphoreType.DMA((16,))],
        compiler_params=pltpu.CompilerParams(vmem_limit_bytes=VMEM_LIMIT),
    )(total, *grads)


def on_device(
    inputs, out_grad, doc_lengths, doc_owner, loss_mask, gain_in, w_in, taps, w_decay, a_log,
    dt_bias, gain_out, w_out, gain_ff, w_ff_in, w_down,
):
    lens, own, mask = (a.reshape(1, TOK) for a in (doc_lengths, doc_owner, loss_mask))
    smalls = (gain_in, gain_ff, gain_out, taps[0].T, w_decay[0].T, a_log, dt_bias)
    mine = (w_in[0], w_out[0], w_ff_in[0], w_down[0])
    out, dx, small, nrm_t, mix_t, nff_t, hid_t, dproj, dmid, dgu, dout = layers(
        inputs, out_grad, mask, lens, own, smalls, mine
    )
    total, *grads = reduce(small, (nrm_t, mix_t, nff_t, hid_t), (dproj, dmid, dgu, dout))
    gin, g_taps, g_wd, g_alog, g_bias, g_gout, g_gff, g_in, g_out, g_ff, g_down = finished(
        total, grads
    )
    return (
        out[None], dx[None], gin, g_in[None], g_taps.T[None], g_wd.T[None], g_alog, g_bias, g_gout,
        g_out[None], g_gff, g_ff[None], g_down[None],
    )


def solution(mesh):
    tokens, pair = P(("dp", "fsdp"), None), P("section", "fsdp")
    matrix = P("section", "fsdp", None)
    params = (pair, matrix, matrix, matrix, pair, pair, pair, matrix, pair, matrix, matrix)
    return jax.shard_map(
        on_device,
        mesh=mesh,
        in_specs=(tokens, tokens, P(), P(), P(("dp", "fsdp")), *params),
        out_specs=(P("section", ("dp", "fsdp"), None),) * 2 + params,
        check_vma=False,
    )
```

time: 2160 us -> 223 us (0.10)
  waiting for transfers between devices: 828 us -> 0 us
  blocking collectives: 698 us -> 0 us
  local copies, waits for them, and re-layouts: 263 us -> 1.42 us
  Pallas kernels: 0 us -> 219 us
  other arithmetic: 204 us -> 0 us
  matrix products: 121 us -> 0 us
    unnamed x15 -> x0, waiting for transfers between devices: 530 us -> none
    all_gather x7 -> x0, blocking collectives: 515 us -> none  [the longest x3 491 us: over_pieces(): blocks = lax.all_gather(x, axis)]
    pallas_call x0 -> x3, Pallas kernels: none -> 219 us  [the longest x1 111 us: layers(): pl.pallas_call(layers_kernel, name='gather_and_layers', out_shape=[jax.Sh...]
    all_gather x9 -> x0, waiting for transfers between devices: 185 us -> none  [the longest x2 151 us: sent_together(): whole = lax.all_gather(both, axis, axis=dim, tiled=True)]
    unnamed x1 -> x0, blocking collectives: 163 us -> none
    another operation x71 -> x0, other arithmetic: 124 us -> none  [the longest x16 79.4 us: advance(): lax.linalg.triangular_solve(system, beta_heads[:, :, None] * value_heads,...]
    ppermute x2 -> x0, waiting for transfers between devices: 113 us -> none  [shifted(): return lax.ppermute(block, axis, route)]
    dot_general x71 -> x0, matrix products: 104 us -> none  [the longest x8 11.5 us: advance(): jnp.einsum('hij,hjv->hiv', scores, state_updates, precision=FINEST_PRECIS...]
  transfers between devices with their start and end apart: 14 -> 0, of which waited for: 8 -> 0; matrix products, arithmetic and copies ran while one was open for 11% -> 0% of each run, Pallas kernels for 0% -> 0%
where the time goes in v1:
time: 223 us; the launch traced here: 221 us
  Pallas kernels  219 us (98%)
    pallas_call x1, Pallas kernels, layers(): pl.pallas_call(layers_kernel, name='gather_and_layers', out_shape=[jax.Sh...  111 us
    pallas_call x1, Pallas kernels, reduce(): pl.pallas_call(functools.partial(reduce_kernel, PAIR_LAG if lag is None e...  98.3 us
    pallas_call x1, Pallas kernels, finished(): pl.pallas_call(finish_kernel, name='widen_gradients', out_shape=[jax.Shap...  9.78 us

profile of v1, /device:TPU:8, one launch (start us, length us, event | category | flops | bytes accessed | tf_op | source)
XLA Modules:
  0.0 221.1 jit_solution(2000265718449219701)
XLA Ops:
  0.7 110.9 %gather_and_layers.1 = (bf16[128,1024]{1,0:T(8,128)(2,1)}, bf16[128,1024]{1,0:T(8,128)(2,1)}, f32[2,80,128]{2,1,0:T(8,128)}, bf16[1024,128]{1,0:T(8,128)(2,1)}, ...) custom-call(bf16[128,1024]{1,0:T(8,128)(2,1)} %x_ref.1, ...), custom_call_target="tpu_custom_call" | custom-call | tf_op jit(solution)/shard_map/gather_and_layers/pallas_call | solution.py:660
  111.5 98.3 %reduce_gradients.1 = (f32[80,128]{1,0:T(8,128)}, bf16[512,3072]{1,0:T(8,128)(2,1)}, bf16[512,1024]{1,0:T(8,128)(2,1)}, bf16[512,2816]{1,0:T(8,128)(2,1)}, bf16[704,1024]{1,0:T(8,128)(2,1)}) custom-call(f32[2,80,128]{2,1,0:T(8,128)} %get-tuple-element.42.small_ref, bf16[1024,128]{1,0:T(8,128)(2,1)} %get-tuple-element.43.l_in, ...), custom_call_target="tpu_custom_call" | custom-call | tf_op jit(solution)/shard_map/reduce_gradients/pallas_call | solution.py:894
  209.8 0.0 copy-start.1
  209.8 0.0 copy-start
  209.8 9.8 %widen_gradients.1 = (f32[1,512]{1,0:T(1,128)}, f32[4,1024]{1,0:T(4,128)}, f32[8,512]{1,0:T(8,128)}, f32[1,2]{1,0:T(1,128)}, f32[1,2]{1,0:T(1,128)}, /*index=5*/...) custom-call(f32[80,128]{1,0:T(8,128)} %get-tuple-element.51.tot_ref,, ...), custom_call_target="tpu_custom_call" | custom-call | tf_op jit(solution)/shard_map/widen_gradients/pallas_call | solution.py:959
  219.6 0.0 copy-done.1
  219.6 0.7 copy.31
  220.4 0.0 copy-done
  220.4 0.7 copy.32
Async XLA Ops:
  209.8 9.8 %copy-start.1 = (bf16[128,1024]{1,0:T(8,128)(2,1)S(1)}, bf16[128,1024]{1,0:T(8,128)(2,1)}, u32[]{:S(2)}) copy-start(bf16[128,1024]{1,0:T(8,128)(2,1)} %get-tuple-element.40) | copy-start | bytes 786436
  209.8 10.5 %copy-start = (bf16[128,1024]{1,0:T(8,128)(2,1)S(1)}, bf16[128,1024]{1,0:T(8,128)(2,1)}, u32[]{:S(2)}) copy-start(bf16[128,1024]{1,0:T(8,128)(2,1)} %get-tuple-element.41) | copy-start | bytes 786436

commit v2 on v1

--- a/solution.py
+++ b/solution.py
@@ -225,7 +225,7 @@
     x_ref, cot_ref, sm_ref, rows_of,
     proj_ref, dec_ref, inv_ref, mid_ref, gu_ref,
     dx_ref, small_ref, nrm_t, mix_t, nff_t, hid_t, dproj_ref, dmid_ref, dgu_ref, dout_ref,
-    w_in, w_out, w_ff, w_down, dmix_ref,
+    w_in, w_out, w_ff, w_down, dmix_ref, hook,
 ):
     i, j = iota(0), iota(1)
     seg_col, seg_row, _ = rows_of
@@ -250,6 +250,7 @@
     n = mid * r
     gain_ff = lanes(sm_ref, R_GFF, 4)
     nff_t[...] = (n * gain_ff).T.astype(BF16)
+    hook("ff")
 
     @pl.loop(0, WIDTH // 256)
     def _(c):
@@ -304,10 +305,10 @@
         d_gain_out = d_gain_out + jnp.sum(dn * nd, axis=0, keepdims=True)
         dn = dn * gain_out
         ddelta = rd * (dn - nd * jnp.mean(dn * nd, axis=-1, keepdims=True))
-        dscores = nt(ddelta, u, M_BWD)
-        du = tn(scores, ddelta, M_BWD)
-        dr = tn(inv, du, M_BWD)
-        da = -nt(dr, u, M_BWD)
+        dscores = nt(ddelta, u, 3)
+        du = tn(scores, ddelta, 3)
+        dr = tn(inv, du, 3)
+        da = -nt(dr, u, 3)
         dqk = dscores * wc
         dgram = da * b * ws
         pair = dqk * qk + dgram * gram
@@ -336,6 +337,7 @@
                 )
                 total = total + pltpu.roll(dcl, TOK - dist, 0) * rows[TAPS - 1 - dist]
             dproj_ref[:, first : first + width] = total.astype(BF16)
+        hook(h)
     put(small_ref, R_GOUT, 1, d_gain_out)
     d_summed = d_col - d_row.T
     later = (j >= i).astype(F32)
@@ -357,6 +359,7 @@
     gain_in = lanes(sm_ref, R_GIN, 4)
     normed = (n * gain_in).astype(BF16)
     nrm_t[...] = (n * gain_in).T.astype(BF16)
+    hook("mixer")
     gwd = tn(ddec, normed)
     for row in range(2 * HEADS):
         put(small_ref, R_WD + 4 * row, 4, gwd[row : row + 1, :])
@@ -388,6 +391,33 @@
 
 ORDERS = ((0, 1, 2, 3), (1, 0, 3, 2), (2, 3, 0, 1), (3, 2, 1, 0))
 FLAT = (
+    (2, 0, 256, 1, False),
+    (2, 256, 768, 3, True),
+    (2, 1024, 768, 2, False),
+    (2, 1792, 1024, 1, True),
+    (3, 0, 1024, 0, False),
+    (0, 0, 1024, 3, False),
+    (0, 1024, 1024, 1, False),
+    (0, 2048, 768, 2, False),
+    (0, 2816, 256, 2, False),
+    (1, 0, 512, 0, True),
+    (1, 512, 512, 2, True),
+)
+ORDER = (
+    (5, 0), (6, 0), (7, 0), (8, 0), (9, 0), (10, 0), (0, 1), (11, 0), (1, 1), (2, 1), (11, 1),
+    (5, 1), (4, 1), (6, 1), (7, 1), (0, 2), (3, 1), (1, 2), (8, 1), (11, 2), (2, 2), (9, 1),
+    (6, 2), (5, 2), (4, 2), (2, 3), (7, 2), (1, 3), (0, 3), (10, 1), (8, 2), (9, 2), (3, 2),
+    (4, 3), (0, 4), (7, 3), (6, 3), (8, 3), (0, 5), (10, 2), (4, 4), (5, 3), (3, 3), (6, 4),
+    (0, 6), (11, 3), (2, 4), (1, 4), (10, 3), (4, 5), (6, 5), (5, 4), (2, 5), (9, 3), (3, 4),
+    (0, 7), (1, 5), (7, 4), (8, 4), (10, 4), (4, 6), (6, 6), (5, 5), (2, 6), (9, 4), (0, 8),
+    (7, 5), (3, 5), (8, 5), (10, 5), (1, 6), (11, 4), (5, 6), (6, 7), (4, 7), (9, 5), (2, 7),
+    (0, 9), (3, 6), (7, 6), (8, 6), (10, 6), (9, 6), (1, 7), (5, 7), (6, 8), (2, 8), (9, 7),
+    (11, 5), (7, 7), (8, 7), (3, 7), (10, 7), (1, 8), (4, 8), (7, 8), (5, 8), (8, 8), (3, 8),
+    (10, 8), (6, 9), (2, 9), (9, 8), (1, 9), (4, 9), (7, 9), (8, 9), (3, 9), (9, 9), (5, 9),
+    (10, 9),
+)
+
+GATHER = (
     (2, 0, 768, 0, True), (2, 768, 768, 1, True), (2, 1536, 768, 3, True), (2, 2304, 512, 2, True),
     (3, 0, 1024, 2, False), (0, 0, 1024, 0, False), (0, 1024, 1024, 1, False),
     (0, 2048, 1024, 3, False), (1, 0, 256, 0, False), (1, 256, 512, 1, False),
@@ -478,20 +508,8 @@
 
 
 GATHER_FLAT = tuple(
-    c[:4] for c in sorted(FLAT, key=lambda c: (0, 3, 1, 2)[c[0]])
+    c[:4] for c in sorted(GATHER, key=lambda c: (0, 3, 1, 2)[c[0]])
 )
-PAIR_LAG = 1.0
-
-
-def in_order(stages, lag):
-    found = []
-    for n, c in enumerate(FLAT):
-        for stage in range(stages):
-            late = lag if c[4] and stage else 0.0
-            found.append((stage + late, n, stage))
-    return [(n, stage) for _, n, stage in sorted(found)]
-
-
 PACKED = 0
 STAGES = 6
 
@@ -499,10 +517,11 @@
 def layers_kernel(
     x_ref, cot_ref, mask_ref, lens_ref, own_ref,
     gin_ref, gff_ref, gout_ref, taps_ref, wdec_ref, alog_ref, bias_ref, wi, wo, wf, wd,
-    out_ref, dx_ref, small_ref, nrm_t, mix_t, nff_t, hid_t, dproj_ref, dmid_ref, dgu_ref, dout_ref,
+    out_ref, dx_ref, tot_ref, g_in, g_out, g_ff, g_down,
+    small_ref, nrm_t, mix_t, nff_t, hid_t, dproj_ref, dmid_ref, dgu_ref, dout_ref,
     w_in, w_out, w_ff, w_down, sm_ref, pk_wide, pk_ref, pk_far, proj_ref, dec_ref, inv_ref,
     mid_ref, gu_ref, mixed_ref, hid_ref, dmix_ref, xin_ref, next_ref, cin_ref, back_ref,
-    send_sem, recv_sem, local_sem,
+    send_sem, recv_sem, local_sem, *scratch,
 ):
     place = Place()
     pk_wide[...] = jnp.zeros_like(pk_wide)
@@ -621,21 +640,46 @@
     )
     cin_ref[...] = (cot_ref[...].astype(F32) * (mask * rows_of[2])).astype(BF16)
 
-    @pl.loop(0, 2)
-    def _(turn):
+    cross, event, small_step, close, sums = reducer(
+        place, (nrm_t, mix_t, nff_t, hid_t), (dproj_ref, dmid_ref, dgu_ref, dout_ref),
+        (g_in, g_out, g_ff, g_down), scratch,
+    )
+
+    def reduce_hook(point):
+        if point == "ff":
+            cross(2)
+            cross(3)
+        elif point == 0:
+            event(0, 0)
+            event(1, 0)
+        elif point == 1:
+            event(2, 0)
+            event(3, 0)
+        elif point == 2:
+            event(4, 0)
+        elif point == "mixer":
+            cross(0)
+            cross(1)
+
+    for turn in range(2):
         backward_body(
             xin_ref, cin_ref, sm_ref, rows_of,
             proj_ref, dec_ref, inv_ref, mid_ref, gu_ref,
             dx_ref, small_ref, nrm_t, mix_t, nff_t, hid_t, dproj_ref, dmid_ref, dgu_ref, dout_ref,
-            w_in, w_out, w_ff, w_down, dmix_ref,
+            w_in, w_out, w_ff, w_down, dmix_ref, reduce_hook if turn else (lambda point: None),
         )
-
-        @pl.when(turn == 0)
-        def _():
+        if turn == 0:
             back.start()
             back.wait()
             cin_ref[...] = jnp.where(section == 0, back_ref[...], cin_ref[...])
 
+    sums[0] = small_ref[...]
+    for n, stage in ORDER:
+        if n == len(FLAT):
+            small_step()
+        else:
+            event(n, stage)
+    close(tot_ref)
     for n in range(count):
         for stage in range(STAGES):
             stage_copy(n, stage).wait_send()
@@ -645,12 +689,14 @@
     vm = pl.BlockSpec(memory_space=pltpu.VMEM)
     hbm = pl.BlockSpec(memory_space=pl.ANY)
     tokens = (TOK, WIDTH)
-    shapes = [
-        (tokens, BF16), (tokens, BF16), ((2, PACK, 128), F32), ((WIDTH, TOK), BF16),
-        ((WIDTH, TOK), BF16), ((WIDTH, TOK), BF16), ((HIDDEN_FF, TOK), BF16), ((TOK, PROJ), BF16),
-        (tokens, BF16), ((TOK, 2 * HIDDEN_FF), BF16), (tokens, BF16),
+    outs = [(tokens, BF16), (tokens, BF16), ((PACK, 128), F32)]
+    outs += [((r, c), BF16) for r, c in zip(HALF_ROWS, COLUMNS)]
+    scratch = [
+        ((2, PACK, 128), F32), ((WIDTH, TOK), BF16), ((WIDTH, TOK), BF16), ((WIDTH, TOK), BF16),
+        ((HIDDEN_FF, TOK), BF16), ((TOK, PROJ), BF16), (tokens, BF16),
+        ((TOK, 2 * HIDDEN_FF), BF16), (tokens, BF16),
     ]
-    scratch = [(s, BF16) for s in WEIGHT_SHAPES] + [
+    scratch += [(s, BF16) for s in WEIGHT_SHAPES] + [
         ((2, PACK, 128), F32), ((PACK, 128), F32), ((PACK, 128), BF16), ((PACK, 128), BF16),
         ((TOK, PROJ), F32), ((TOK, TOK), F32), ((HEADS, TOK, TOK), F32), (tokens, F32),
         ((TOK, 2 * HIDDEN_FF), F32), (tokens, BF16), ((TOK, HIDDEN_FF), BF16), (tokens, F32),
@@ -659,29 +705,24 @@
     count = 3 + STAGES * len(GATHER_FLAT)
     return pl.pallas_call(
         layers_kernel,
-        name="gather_and_layers",
-        out_shape=[jax.ShapeDtypeStruct(s, d) for s, d in shapes],
+        name="layers_and_sums",
+        out_shape=[jax.ShapeDtypeStruct(s, d) for s, d in outs],
         in_specs=[vm] * 12 + [hbm] * 4,
-        out_specs=[vm] * len(shapes),
+        out_specs=[vm] * 3 + [hbm] * 4,
         scratch_shapes=[pltpu.VMEM(s, d) for s, d in scratch]
         + [
             pltpu.SemaphoreType.DMA((count,)),
             pltpu.SemaphoreType.DMA((count,)),
             pltpu.SemaphoreType.DMA((4,)),
-        ],
+        ]
+        + reducer_scratch(),
         compiler_params=pltpu.CompilerParams(
             collective_id=1, has_side_effects=True, vmem_limit_bytes=VMEM_LIMIT
         ),
     )(x, cot, mask, lens, own, *smalls, *weights)
 
 
-def reduce_kernel(
-    lag, stages, small_ref, l_in, l_out, l_ff, l_down, r_in, r_out, r_ff, r_down,
-    tot_ref, g_in, g_out, g_ff, g_down, *scratch,
-):
-    place = Place()
-    lhs, rhs = (l_in, l_out, l_ff, l_down), (r_in, r_out, r_ff, r_down)
-    grads = (g_in, g_out, g_ff, g_down)
+def reducer(place, lhs, rhs, grads, scratch):
     peer_l, peer_r = scratch[0:4], scratch[4:8]
     count = len(FLAT)
     parts, fins = scratch[8 : 8 + count], scratch[8 + count : 8 + 2 * count]
@@ -690,11 +731,11 @@
     sums, sums_in, sums_pair, send_sem, recv_sem, local_sem = scratch[5 * count :]
     sems = (send_sem, recv_sem)
     ids = iter(range(10 * count + 18))
-    place.greet()
-    sent = []
-
+    chunks = [Chunk(place, *c) for c in FLAT]
+    last, local, sent = {}, {}, []
     crossing = {}
-    for w in (2, 3, 0, 1):
+
+    def cross(w):
         rows = peer_l[w].shape[1]
         found = []
         for h in range(2):
@@ -703,17 +744,9 @@
                 send(lhs[w].at[pl.ds(at, rows), :], peer_l[w].at[h], sems, next(ids), place.sibling)
             )
         found.append(send(rhs[w], peer_r[w], sems, next(ids), place.sibling))
-        sent += found
+        sent.extend(found)
         crossing[w] = found
 
-    sums[0] = small_ref[...]
-    steps = (place.sibling, *place.links)
-    small_ids = [next(ids) for _ in range(6)]
-    small = send(sums.at[0], sums_in.at[0], sems, small_ids[0], steps[0])
-    sent.append(small)
-
-    chunks = [Chunk(place, *c) for c in FLAT]
-    last, local = {}, {}
 
     def product(n, first):
         c = chunks[n]
@@ -778,7 +811,7 @@
         last[n] = send(src, dst, sems, next(ids), place.pair)
         sent.append(last[n])
 
-    for n, stage in in_order(stages, lag):
+    def event(n, stage):
         c = chunks[n]
         w = c.weight
         if stage == 0:
@@ -846,22 +879,33 @@
             block = grads[w].at[c.window(0, row0=place.core * c.rows, col0=c.first)]
             last[n] = send(block, block, sems, next(ids), place.sibling)
             sent.append(last[n])
-        if stage == 0 and 1 <= n <= 5:
-            small.wait_recv()
-            sums[n] = sums[n - 1] + sums_in[n - 1]
-            if n < 5:
-                small = send(sums.at[n], sums_in.at[n], sems, small_ids[n], steps[n])
-            else:
-                small = send(
-                    sums.at[5, 1 - place.half], sums_pair, sems, small_ids[5], place.pair
-                )
-            sent.append(small)
-    small.wait_recv()
-    tot_ref[...] = sums[5, place.half] + sums_pair[...]
-    for n in range(count):
-        last[n].wait_recv()
-    for copy in sent:
-        copy.wait_send()
+
+    small = []
+
+    def small_step():
+        steps = (place.sibling, *place.links)
+        k = len(small)
+        if 0 < k < 6:
+            small[-1].wait_recv()
+            sums[k] = sums[k - 1] + sums_in[k - 1]
+        if k < 5:
+            small.append(send(sums.at[k], sums_in.at[k], sems, next(ids), steps[k]))
+        elif k == 5:
+            small.append(
+                send(sums.at[5, 1 - place.half], sums_pair, sems, next(ids), place.pair)
+            )
+
+    def close(tot_ref):
+        while len(small) < 6:
+            small_step()
+        small[-1].wait_recv()
+        tot_ref[...] = sums[5, place.half] + sums_pair[...]
+        for n in range(count):
+            last[n].wait_recv()
+        for copy in sent + small:
+            copy.wait_send()
+
+    return cross, event, small_step, close, sums
 
 
 class Sizes:
@@ -869,9 +913,7 @@
     links = (None,) * 4
 
 
-def reduce(small, lhs, rhs, lag=None, stages=10, cid=2):
-    vm = pl.BlockSpec(memory_space=pltpu.VMEM)
-    hbm = pl.BlockSpec(memory_space=pl.ANY)
+def reducer_scratch():
     chunks = [Chunk(Sizes, *c) for c in FLAT]
     count = len(FLAT)
     scratch = [pltpu.VMEM((2, r // 2, TOK), BF16) for r in HALF_ROWS]
@@ -891,24 +933,14 @@
         pltpu.SemaphoreType.DMA((total,)),
         pltpu.SemaphoreType.DMA((count,)),
     ]
-    return pl.pallas_call(
-        functools.partial(reduce_kernel, PAIR_LAG if lag is None else lag, stages),
-        name="reduce_gradients",
-        out_shape=[jax.ShapeDtypeStruct((PACK, 128), F32)]
-        + [jax.ShapeDtypeStruct((r, c), BF16) for r, c in zip(HALF_ROWS, COLUMNS)],
-        in_specs=[vm] * 9,
-        out_specs=[vm] + [hbm] * 4,
-        scratch_shapes=scratch,
-        compiler_params=pltpu.CompilerParams(
-            collective_id=cid, has_side_effects=True, vmem_limit_bytes=VMEM_LIMIT
-        ),
-    )(small, *lhs, *rhs)
-
-
-def finish_kernel(tot_ref, *refs):
+    return scratch
+
+
+def finish_kernel(tot_ref, out_ref, dx_ref, *refs):
     sources, (o_gin, o_taps, o_wd, o_alog, o_bias, o_gout, o_gff) = refs[:4], refs[4:11]
-    targets, narrow, wide = refs[11:15], refs[15:19], refs[19:23]
-    in_sem, out_sem = refs[23:]
+    targets, o_out, o_dx = refs[11:15], refs[15], refs[16]
+    narrow, wide = refs[17:21], refs[21:25]
+    t_out, t_dx, in_sem, out_sem = refs[25:]
     half = lax.axis_index("fsdp")
     blocks = []
     for w, rows in enumerate(HALF_ROWS):
@@ -920,6 +952,12 @@
     ]
     for copy in loads:
         copy.start()
+    tokens = ((out_ref, t_out, o_out), (dx_ref, t_dx, o_dx))
+    passing = [
+        pltpu.make_async_copy(src, via, in_sem.at[16 + k]) for k, (src, via, _) in enumerate(tokens)
+    ]
+    for copy in passing:
+        copy.start()
 
     def row(first, count):
         return jnp.concatenate([tot_ref[first + k : first + k + 1, :] for k in range(count)], 1)
@@ -935,6 +973,10 @@
         both = row(at, 1)
         ref[...] = jnp.where(half == 0, both[:, 0:2], both[:, 2:4])
     stores = []
+    for k, (_, via, dst) in enumerate(tokens):
+        passing[k].wait()
+        stores.append(pltpu.make_async_copy(via, dst, out_sem.at[16 + k]))
+        stores[-1].start()
     for k, (w, at) in enumerate(blocks):
         loads[k].wait()
         first, count = at.start, at.stop - at.start
@@ -951,7 +993,7 @@
         copy.wait()
 
 
-def finished(total, grads):
+def finished(total, out, dx, grads):
     vm = pl.BlockSpec(memory_space=pltpu.VMEM)
     hbm = pl.BlockSpec(memory_space=pl.ANY)
     small = [(1, 512), (TAPS, 1024), (2 * HEADS, 512), (1, 2), (1, 2), (1, 128), (1, 512)]
@@ -959,14 +1001,16 @@
     return pl.pallas_call(
         finish_kernel,
         name="widen_gradients",
-        out_shape=[jax.ShapeDtypeStruct(s, F32) for s in small + shapes],
-        in_specs=[vm] + [hbm] * 4,
-        out_specs=[vm] * 7 + [hbm] * 4,
+        out_shape=[jax.ShapeDtypeStruct(s, F32) for s in small + shapes]
+        + [jax.ShapeDtypeStruct((TOK, WIDTH), BF16)] * 2,
+        in_specs=[vm] + [hbm] * 6,
+        out_specs=[vm] * 7 + [hbm] * 6,
         scratch_shapes=[pltpu.VMEM(s, BF16) for s in shapes]
         + [pltpu.VMEM(s, F32) for s in shapes]
-        + [pltpu.SemaphoreType.DMA((16,)), pltpu.SemaphoreType.DMA((16,))],
+        + [pltpu.VMEM((TOK, WIDTH), BF16)] * 2
+        + [pltpu.SemaphoreType.DMA((18,)), pltpu.SemaphoreType.DMA((18,))],
         compiler_params=pltpu.CompilerParams(vmem_limit_bytes=VMEM_LIMIT),
-    )(total, *grads)
+    )(total, out, dx, *grads)
 
 
 def on_device(
@@ -976,12 +1020,9 @@
     lens, own, mask = (a.reshape(1, TOK) for a in (doc_lengths, doc_owner, loss_mask))
     smalls = (gain_in, gain_ff, gain_out, taps[0].T, w_decay[0].T, a_log, dt_bias)
     mine = (w_in[0], w_out[0], w_ff_in[0], w_down[0])
-    out, dx, small, nrm_t, mix_t, nff_t, hid_t, dproj, dmid, dgu, dout = layers(
-        inputs, out_grad, mask, lens, own, smalls, mine
-    )
-    total, *grads = reduce(small, (nrm_t, mix_t, nff_t, hid_t), (dproj, dmid, dgu, dout))
-    gin, g_taps, g_wd, g_alog, g_bias, g_gout, g_gff, g_in, g_out, g_ff, g_down = finished(
-        total, grads
+    out, dx, total, *grads = layers(inputs, out_grad, mask, lens, own, smalls, mine)
+    gin, g_taps, g_wd, g_alog, g_bias, g_gout, g_gff, g_in, g_out, g_ff, g_down, out, dx = finished(
+        total, out, dx, grads
     )
     return (
         out[None], dx[None], gin, g_in[None], g_taps.T[None], g_wd.T[None], g_alog, g_bias, g_gout,

time: 223 us -> 203 us (0.910)
  Pallas kernels: 219 us -> 200 us
    pallas_call x2 -> x1, Pallas kernels: 209 us -> 189 us  [layers(): pl.pallas_call(layers_kernel, name='layers_and_sums', out_shape=[jax.Shap...]
where the time goes in v2:
time: 203 us; the launch traced here: 201 us
  Pallas kernels  200 us (99%)
    pallas_call x1, Pallas kernels, layers(): pl.pallas_call(layers_kernel, name='layers_and_sums', out_shape=[jax.Shap...  189 us
    pallas_call x1, Pallas kernels, finished(): pl.pallas_call(finish_kernel, name='widen_gradients', out_shape=[jax.Shap...  11.3 us

profile of v2, /device:TPU:8, one launch (start us, length us, event | category | flops | bytes accessed | tf_op | source)
XLA Modules:
  0.0 201.3 jit_solution(7540613130225973806)
XLA Ops:
  0.7 189.1 %layers_and_sums.1 = (bf16[128,1024]{1,0:T(8,128)(2,1)}, bf16[128,1024]{1,0:T(8,128)(2,1)}, f32[80,128]{1,0:T(8,128)}, bf16[512,3072]{1,0:T(8,128)(2,1)}, bf16[5...) custom-call(bf16[128,1024]{1,0:T(8,128)(2,1)} %x_ref.1, bf16[128,1024]{1,0:T(8,128)(2,1)} %cot_ref.1, ...), custom_call_target="tpu_custom_call" | custom-call | tf_op jit(solution)/shard_map/layers_and_sums/pallas_call | solution.py:706
  189.8 11.3 %widen_gradients.1 = (f32[1,512]{1,0:T(1,128)}, f32[4,1024]{1,0:T(4,128)}, f32[8,512]{1,0:T(8,128)}, f32[1,2]{1,0:T(1,128)}, f32[1,2]{1,0:T(1,128)}, /*index=5*/...) custom-call(f32[80,128]{1,0:T(8,128)} %get-tuple-element.33.tot_ref,, ...), custom_call_target="tpu_custom_call" | custom-call | tf_op jit(solution)/shard_map/widen_gradients/pallas_call | solution.py:1001

commit v3 on v2

--- a/solution.py
+++ b/solution.py
@@ -166,10 +166,8 @@
     dec_ref[...] = dec
     hook("in")
 
-    @pl.loop(0, PROJ // 512)
-    def _(c):
-        cols = pl.ds(pl.multiple_of(c * 512, 512), 512)
-        proj_ref[:, cols] = nn(normed, w_in[:, cols])
+    for c in range(0, PROJ, 512):
+        proj_ref[:, c : c + 512] = nn(normed, w_in[:, c : c + 512])
 
     z, rate, logdecay, summed, beta = decays(dec, sm_ref)
     summed_t = summed.T
@@ -207,10 +205,10 @@
     normed_ff = (mid * norm_rows(mid) * lanes(sm_ref, R_GFF, 4)).astype(BF16)
     hook("ff")
 
-    @pl.loop(0, HIDDEN_FF // 128)
-    def _(c):
-        a = pl.ds(pl.multiple_of(c * 128, 128), 128)
-        b = pl.ds(pl.multiple_of(HIDDEN_FF + c * 128, 128), 128)
+    for first in range(0, HIDDEN_FF, 256):
+        width = min(256, HIDDEN_FF - first)
+        a = slice(first, first + width)
+        b = slice(HIDDEN_FF + first, HIDDEN_FF + first + width)
         gate = nn(normed_ff, w_ff[:, a])
         up = nn(normed_ff, w_ff[:, b])
         gu_ref[:, a] = gate
@@ -236,9 +234,10 @@
     dout_ref[...] = doutb
     small_ref[...] = jnp.zeros_like(small_ref)
 
-    for c in range(HIDDEN_FF // 128):
-        a = slice(c * 128, c * 128 + 128)
-        b = slice(HIDDEN_FF + c * 128, HIDDEN_FF + c * 128 + 128)
+    for first in range(0, HIDDEN_FF, 256):
+        width = min(256, HIDDEN_FF - first)
+        a = slice(first, first + width)
+        b = slice(HIDDEN_FF + first, HIDDEN_FF + first + width)
         gate, up = gu_ref[:, a], gu_ref[:, b]
         sg = sigmoid(gate)
         d_hidden = nt(doutb, w_down[a, :])
@@ -252,10 +251,8 @@
     nff_t[...] = (n * gain_ff).T.astype(BF16)
     hook("ff")
 
-    @pl.loop(0, WIDTH // 256)
-    def _(c):
-        rows = pl.ds(pl.multiple_of(c * 256, 256), 256)
-        dmix_ref[:, rows] = nt(dgu_ref[...], w_ff[rows, :])
+    for c in range(0, WIDTH, 256):
+        dmix_ref[:, c : c + 256] = nt(dgu_ref[...], w_ff[c : c + 256, :])
 
     d = dmix_ref[...]
     put(small_ref, R_GFF, 4, jnp.sum(d * n, axis=0, keepdims=True))
@@ -364,10 +361,8 @@
     for row in range(2 * HEADS):
         put(small_ref, R_WD + 4 * row, 4, gwd[row : row + 1, :])
 
-    @pl.loop(0, WIDTH // 256)
-    def _(c):
-        rows = pl.ds(pl.multiple_of(c * 256, 256), 256)
-        dmix_ref[:, rows] = nt(dproj_ref[...], w_in[rows, :])
+    for c in range(0, WIDTH, 256):
+        dmix_ref[:, c : c + 256] = nt(dproj_ref[...], w_in[c : c + 256, :])
 
     d = dmix_ref[...] + nn(ddec, decay_weights(sm_ref))
     put(small_ref, R_GIN, 4, jnp.sum(d * n, axis=0, keepdims=True))

time: 203 us -> 196 us (0.966)
  Pallas kernels: 200 us -> 192 us
    pallas_call x1, Pallas kernels: 189 us -> 181 us  [layers(): pl.pallas_call(layers_kernel, name='layers_and_sums', out_shape=[jax.Shap...]
where the time goes in v3:
time: 196 us; the launch traced here: 193 us
  Pallas kernels  192 us (98%)
    pallas_call x1, Pallas kernels, layers(): pl.pallas_call(layers_kernel, name='layers_and_sums', out_shape=[jax.Shap...  181 us
    pallas_call x1, Pallas kernels, finished(): pl.pallas_call(finish_kernel, name='widen_gradients', out_shape=[jax.Shap...  11.3 us

profile of v3, /device:TPU:8, one launch (start us, length us, event | category | flops | bytes accessed | tf_op | source)
XLA Modules:
  0.0 193.3 jit_solution(17470065201884250401)
XLA Ops:
  0.7 181.2 %layers_and_sums.1 = (bf16[128,1024]{1,0:T(8,128)(2,1)}, bf16[128,1024]{1,0:T(8,128)(2,1)}, f32[80,128]{1,0:T(8,128)}, bf16[512,3072]{1,0:T(8,128)(2,1)}, bf16[5...) custom-call(bf16[128,1024]{1,0:T(8,128)(2,1)} %x_ref.1, bf16[128,1024]{1,0:T(8,128)(2,1)} %cot_ref.1, ...), custom_call_target="tpu_custom_call" | custom-call | tf_op jit(solution)/shard_map/layers_and_sums/pallas_call | solution.py:701
  181.8 11.3 %widen_gradients.1 = (f32[1,512]{1,0:T(1,128)}, f32[4,1024]{1,0:T(4,128)}, f32[8,512]{1,0:T(8,128)}, f32[1,2]{1,0:T(1,128)}, f32[1,2]{1,0:T(1,128)}, /*index=5*/...) custom-call(f32[80,128]{1,0:T(8,128)} %get-tuple-element.33.tot_ref,, ...), custom_call_target="tpu_custom_call" | custom-call | tf_op jit(solution)/shard_map/widen_gradients/pallas_call | solution.py:996
